TPU v7x, 256 devices: a whole 4x4x8 slice. The times are simulated.
256 devices in a mesh: win: 32 (over z, x_lo, core), head: 8 (over y, x_hi).
Axes of the slice: x: 4 (x_hi: 2, x_lo: 2; x = x_hi * 2 + x_lo), y: 4, z: 8, core: 2. Of those that a mesh axis runs over, the one named last changes fastest.
Arguments:
- query_tokens: bfloat16 [32, 1152, 5120], P('win', None, 'head'), may hold values from -20 to 20
- key_tokens: bfloat16 [32, 1152, 5120], P('win', None, 'head'), may hold values from -20 to 20
- value_tokens: bfloat16 [32, 1152, 5120], P('win', None, 'head'), may hold values from -6 to 6
- context_index: int32 [32, 16], replicated, may hold values from -1 to 383, as said below
- window_start: int32 [32], replicated, may hold values from 0 to 255, as said below
Outputs:
- blended_out: bfloat16 [32, 1152, 5120], P('win', None, 'head')
Inputs may be any that keep to these rules, and one draw needn't show every extreme that they name: `context_index`: -1 marks an unused slot. The used slots of a window name distinct windows other than itself, always include a frame of each of the next two windows (counted round the end), and number 2 to 16, 16 in some window and 2 in another. The frames named of any one window are exactly 2 distinct ones; the last frame of the last window is named. `window_start`: window w starts at a position from w * 8 to w * 8 + 7; the first window starts at 0 and the last at the end of its range.
All inputs are finite; a program needn't handle non-finite values.
Results may differ from a plain program's by a relative error of at most 0.0046.
Values may be sent and summed in bfloat16 or wider, within the bound.
No kernel may reach another device: no remote copies, remote signals or barrier semaphores. Data moves between devices by JAX's collectives and lax.ppermute only.
A program may use at most 128 MiB of HBM per device.

v0:
```python
import math

import jax
import jax.numpy as jnp
from jax import lax
from jax.sharding import PartitionSpec as P

HEADS = 40
HD = 128
FT = 96
WF = 12
SF = 4
OWE = 2


def shifted(value, axis, by):
    peers = lax.axis_size(axis)
    pairs = [(i, i + by) for i in range(peers) if 0 <= i + by < peers]
    return lax.ppermute(value, axis, pairs)


def head_mix(scores, values):
    top_score = jnp.max(scores, axis=-1, keepdims=True)
    exponent = jnp.exp(scores - top_score)
    totals = jnp.sum(exponent, axis=-1, keepdims=True)
    weights = exponent.astype(jnp.bfloat16)
    return jnp.dot(weights, values, preferred_element_type=jnp.float32) / totals


def cross_mix(queries, keys_part, values_part, heads_here, score_scale):
    n_rows = queries.shape[0]
    q_split = queries.reshape(n_rows, heads_here, HD)
    k_split = keys_part.reshape(n_rows, heads_here, HD)
    v_split = values_part.reshape(n_rows, heads_here, HD)
    scores = (
        jnp.einsum("qhd,khd->hqk", q_split, k_split, preferred_element_type=jnp.float32)
        * score_scale
    )
    top_score = jnp.max(scores, axis=-1, keepdims=True)
    exponent = jnp.exp(scores - top_score)
    totals = jnp.sum(exponent, axis=-1, keepdims=True)
    weights = exponent.astype(jnp.bfloat16)
    return jnp.einsum("hqk,khd->hqd", weights, v_split, preferred_element_type=jnp.float32) / totals


def on_device(query_tokens, key_tokens, value_tokens, context_index, window_start):
    row_count = query_tokens.shape[1]
    feat_dev = query_tokens.shape[2]
    heads_here = feat_dev // HD
    ctx_slots = context_index.shape[1]
    shared = SF * FT
    windows = lax.axis_size("win")
    win_id = lax.axis_index("win")
    head_base = lax.axis_index("head") * heads_here
    score_scale = 1.0 / math.sqrt(HD)
    slopes = 0.25 * jnp.exp2(
        -8.0 * (head_base + jnp.arange(heads_here, dtype=jnp.int32)).astype(jnp.float32) / HEADS
    )
    queries = query_tokens[0]
    keys_own = key_tokens[0]
    values_own = value_tokens[0]
    is_live = context_index >= 0
    safe_idx = jnp.maximum(context_index, 0)
    source = safe_idx // WF
    frame_idx = safe_idx % WF
    my_live = lax.dynamic_index_in_dim(is_live, win_id, 0, keepdims=False)
    my_source = lax.dynamic_index_in_dim(source, win_id, 0, keepdims=False)
    my_frame = lax.dynamic_index_in_dim(frame_idx, win_id, 0, keepdims=False)
    key_frames = keys_own.reshape(WF, FT, feat_dev)
    value_frames = values_own.reshape(WF, FT, feat_dev)
    win_range = jnp.arange(windows, dtype=jnp.int32)
    frame_range = jnp.arange(WF, dtype=jnp.int32)
    asked_me = is_live & (source == win_id)
    source_table = my_source[:, None] == win_range[None, :]
    low_own = jnp.min(jnp.where(asked_me, frame_idx, WF))
    high_own = jnp.max(jnp.where(asked_me, frame_idx, -1))
    packer = (frame_range[None, :] == jnp.stack([low_own, high_own])[:, None]).astype(jnp.bfloat16)
    pack_keys = jnp.einsum(
        "ow,wtf->otf", packer, key_frames, preferred_element_type=jnp.float32
    ).astype(jnp.bfloat16)
    pack_values = jnp.einsum(
        "ow,wtf->otf", packer, value_frames, preferred_element_type=jnp.float32
    ).astype(jnp.bfloat16)
    naming = is_live[:, :, None] & (source[:, :, None] == win_range[None, None, :])
    low_all = jnp.min(jnp.where(naming, frame_idx[:, :, None], WF), axis=(0, 1))
    high_all = jnp.max(jnp.where(naming, frame_idx[:, :, None], -1), axis=(0, 1))
    my_low = jnp.sum(jnp.where(source_table, low_all[None, :], 0), axis=1)
    my_high = jnp.sum(jnp.where(source_table, high_all[None, :], 0), axis=1)
    is_upper = (my_frame == my_high) & (my_high != my_low)
    target = my_source * OWE + is_upper.astype(jnp.int32)
    blank_buf = jnp.zeros((ctx_slots, FT, feat_dev), jnp.bfloat16)
    portion = (
        lax.all_gather(pack_keys, "win", axis=0, tiled=True),
        lax.all_gather(pack_values, "win", axis=0, tiled=True),
    )
    span_len = portion[0].shape[0]
    inside = (target >= 0) & (target < span_len)
    selector = (target[:, None] == jnp.arange(span_len, dtype=jnp.int32)[None, :]).astype(
        jnp.bfloat16
    )
    new_keys = jnp.einsum(
        "cn,ntf->ctf", selector, portion[0], preferred_element_type=jnp.float32
    ).astype(jnp.bfloat16)
    new_values = jnp.einsum(
        "cn,ntf->ctf", selector, portion[1], preferred_element_type=jnp.float32
    ).astype(jnp.bfloat16)
    ctx_keys = jnp.where(inside[:, None, None], new_keys, blank_buf)
    ctx_values = jnp.where(inside[:, None, None], new_values, blank_buf)
    key_pos = jnp.sum(jnp.where(source_table, window_start[None, :], 0), axis=1) + my_frame
    query_pos = (
        lax.dynamic_index_in_dim(window_start, win_id, 0, keepdims=False)
        + jnp.arange(row_count, dtype=jnp.int32) // FT
    )
    distance = jnp.repeat(
        jnp.abs(query_pos[:, None] - key_pos[None, :]).astype(jnp.float32), FT, axis=1
    )
    key_live = jnp.repeat(my_live, FT)
    all_keys = jnp.concatenate([keys_own, ctx_keys.reshape(ctx_slots * FT, feat_dev)], axis=0)
    all_values = jnp.concatenate([values_own, ctx_values.reshape(ctx_slots * FT, feat_dev)], axis=0)
    key_heads = all_keys.reshape(-1, heads_here, HD).transpose(1, 0, 2)
    value_heads = all_values.reshape(-1, heads_here, HD).transpose(1, 0, 2)
    query_heads = queries.reshape(row_count, heads_here, HD).transpose(1, 0, 2)

    def one_head(head_id):
        q_one = query_heads[head_id]
        k_one = key_heads[head_id]
        v_one = value_heads[head_id]
        scores = (
            lax.dot_general(
                q_one, k_one, (((1,), (1,)), ((), ())), preferred_element_type=jnp.float32
            )
            * score_scale
        )
        ctx_bias = jnp.where(key_live[None, :], -slopes[head_id] * distance, -jnp.inf)
        scores = jnp.concatenate([scores[:, :row_count], scores[:, row_count:] + ctx_bias], axis=1)
        return head_mix(scores, v_one)

    blended = lax.map(one_head, jnp.arange(heads_here, dtype=jnp.int32))
    left_keys, left_values = shifted(
        (keys_own[row_count - shared :], values_own[row_count - shared :]), "win", 1
    )
    right_keys, right_values = shifted((keys_own[:shared], values_own[:shared]), "win", -1)
    cross_head = cross_mix(queries[:shared], left_keys, left_values, heads_here, score_scale)
    cross_tail = cross_mix(
        queries[row_count - shared :], right_keys, right_values, heads_here, score_scale
    )
    step_in = (jnp.arange(shared, dtype=jnp.int32) // FT).astype(jnp.float32)
    beta_head = jnp.where(win_id > 0, (step_in + 1.0) / (SF + 1.0), 1.0)[None, :, None]
    beta_tail = jnp.where(win_id < windows - 1, (SF - step_in) / (SF + 1.0), 1.0)[None, :, None]
    head_rows = beta_head * blended[:, :shared] + (1.0 - beta_head) * cross_head
    tail_rows = beta_tail * blended[:, row_count - shared :] + (1.0 - beta_tail) * cross_tail
    joined = jnp.concatenate(
        [head_rows, blended[:, shared : row_count - shared], tail_rows], axis=1
    )
    return joined.transpose(1, 0, 2).reshape(1, row_count, feat_dev).astype(jnp.bfloat16)


def solution(mesh):
    return jax.shard_map(
        on_device,
        mesh=mesh,
        in_specs=(P("win", None, "head"), P("win", None, "head"), P("win", None, "head"), P(), P()),
        out_specs=P("win", None, "head"),
        check_vma=False,
    )
```

profile of v0, /device:TPU:1, one launch (start us, length us, event | category | flops | bytes accessed | tf_op | source)
XLA Modules:
  0.0 397.5 jit_solution(9385017056998034766)
XLA Ops:
  15.8 4.5 %collective-permute-start = (bf16[384,640]{0,1:T(8,128)(2,1)}, bf16[384,640]{0,1:T(8,128)(2,1)}, u32[]{:S(2)}, u32[]{:S(2)}) collective-permute-start(bf16[384,640]{0,1:T(8,128)(2,1)} %get-tuple-element.137), channel_id=1, source_target_pairs={{0,8},{8,16},{16,24},{24,32},{32,40},{40,48},{48,56},{56,64},{64,7... | collective-permute-start | bytes 1474568 | tf_op jit(solution)/shard_map/ppermute | solution.py:19
  46.7 47.5 %all-gather.3.cloned.1.call-done = bf16[64,96,640]{2,1,0:T(8,128)(2,1)} async-done(((bf16[2,96,640]{2,1,0:T(8,128)(2,1)}), bf16[64,96,640]{2,1,0:T(8,128)(2,1)}) %all-gather.3.cloned.1.call-update) | async-done | bytes 7864336 | tf_op jit(solution)/shard_map/all_gather | solution.py:93
  94.2 7.3 %convert_select_fusion.1 = bf16[16,96,640]{2,0,1:T(8,128)(2,1)} fusion(pred[16]{0:T(512)(128)(4,1)S(1)} %get-tuple-element.133, bf16[64,96,640]{2,1,0:T(8,128)(2,1)} %all-gather.3.cloned.1.call-done, s32[16]{0:T(128)S(1)} %get-tuple-element.134), kind=kOutput, calls=%fused_computation.41 | convolution fusion | flops 127796224 | bytes 9830480 | tf_op jit(solution)/shard_map/cn,ntf->ctf/dot_general | solution.py:101
  101.5 4.5 %copy.78 = bf16[16,96,640]{1,0,2:T(8,128)(2,1)S(1)} copy(bf16[16,96,640]{2,0,1:T(8,128)(2,1)} %convert_select_fusion.1) | data formatting | bytes 3932160 | tf_op jit(solution)/shard_map/jit(_where)/select_n | solution.py:107
  106.0 3.8 concatenate.24
  109.8 57.9 %all-gather.5.cloned.1.call-done = bf16[64,96,640]{2,1,0:T(8,128)(2,1)} async-done(((bf16[2,96,640]{2,1,0:T(8,128)(2,1)}), bf16[64,96,640]{2,1,0:T(8,128)(2,1)}) %all-gather.5.cloned.1.call-update) | async-done | bytes 7864336 | tf_op jit(solution)/shard_map/all_gather | solution.py:94
  167.7 7.3 %convert_select_fusion = bf16[16,96,640]{2,0,1:T(8,128)(2,1)} fusion(pred[16]{0:T(512)(128)(4,1)S(1)} %get-tuple-element.133, bf16[64,96,640]{2,1,0:T(8,128)(2,1)} %all-gather.5.cloned.1.call-done, s32[16]{0:T(128)S(1)} %get-tuple-element.134), kind=kOutput, calls=%fused_computation.40 | convolution fusion | flops 127796224 | bytes 9830480 | tf_op jit(solution)/shard_map/cn,ntf->ctf/dot_general | solution.py:104
  175.0 4.5 %copy.83 = bf16[16,96,640]{1,0,2:T(8,128)(2,1)S(1)} copy(bf16[16,96,640]{2,0,1:T(8,128)(2,1)} %convert_select_fusion) | data formatting | bytes 3932160 | tf_op jit(solution)/shard_map/jit(_where)/select_n | solution.py:108
  179.5 3.8 concatenate.27
  188.4 191.9 %while.11 = (s32[]{:T(128)}, f32[5,1152,128]{2,1,0:T(8,128)}, s32[5]{0:T(128)S(1)}, bf16[5,1152,128]{1,2,0:T(8,128)(2,1)}, bf16[5,2688,128]{1,2,0:T(8,128)(2,1)S...) while((s32[]{:T(128)}, f32[5,1152,128]{2,1,0:T(8,128)}, ...), condition=%wide.region_11.12_spmd.clone, body=%wide.region_7.11_spmd.clone.sunk | while | flops 1615673088 | bytes 92627488 | solution.py:138
  190.7 7.3 %convolution_multiply_fusion.2 = f32[1152,2688]{1,0:T(8,128)} fusion(bf16[5,2688,128]{1,2,0:T(8,128)(2,1)S(1)} %get-tuple-element.243, s32[]{:T(128)S(6)} %select_n.184, bf16[5,1152,128]{1,2,0:T(8,128)(2,1)} %get-tuple-element.242), kind=kOutput, calls=%fused_computation.2.clone.1 | convolution fusion | flops 795820032 | bytes 13370368 | tf_op jit(solution)/shard_map/while/body/eval_jaxpr/dot_general | solution.py:129
  199.3 3.4 broadcast_in_dim.160
  202.7 8.0 %copy.131 = f32[1152,1536]{1,0:T(8,128)} copy(f32[1152,1536]{0,1:T(8,128)} %bitcast.98) | data formatting | bytes 14155776 | tf_op jit(solution)/shard_map/reshape | solution.py:114
  210.9 6.1 %fusion.125 = (f32[1152]{0:T(1024)S(1)}, f32[1152,1536]{1,0:T(8,128)S(1)}) fusion(f32[1152,1536]{1,0:T(8,128)} %copy.131, f32[]{:T(128)} %bitcast.97, pred[1536]{0:T(1024)(128)(4,1)S(1)} %broadcast_in_dim.162, f32[1152,2688]{1,0:T(8,128)} %convolution_multiply_fusion.2), kind=kLoop, calls=%fused_computation.124.clone.1 | loop fusion | flops 7076736 | bytes 21239812 | tf_op jit(solution)/shard_map/while/body/eval_jaxpr/reduce_max | solution.py:23
  222.4 4.4 %fusion.127 = f32[5,1152,128]{2,1,0:T(8,128)} fusion(f32[5,1152,128]{2,1,0:T(8,128)} %get-tuple-element.228, s32[]{:T(128)} %get-tuple-element.227, f32[1152,1536]{1,0:T(8,128)S(1)} %get-tuple-element.211, f32[1152,1152]{1,0:T(8,128)S(1)} %get-tuple-element.212, f32[1152]{0:T(1024)S(1)} %reduce_max.74, ...), kind=kOutput, calls=%fused_computation.11.clone.1 | convolution fusion | flops 802160640 | bytes 13673988 | tf_op jit(solution)/shard_map/while/body/eval_jaxpr/dot_general | solution.py:27
  229.0 7.3 %convolution_multiply_fusion.2 = f32[1152,2688]{1,0:T(8,128)} fusion(bf16[5,2688,128]{1,2,0:T(8,128)(2,1)S(1)} %get-tuple-element.243, s32[]{:T(128)S(6)} %select_n.184, bf16[5,1152,128]{1,2,0:T(8,128)(2,1)} %get-tuple-element.242), kind=kOutput, calls=%fused_computation.2.clone.1 | convolution fusion | flops 795820032 | bytes 13370368 | tf_op jit(solution)/shard_map/while/body/eval_jaxpr/dot_general | solution.py:129
  237.7 3.4 broadcast_in_dim.160
  241.1 8.0 %copy.131 = f32[1152,1536]{1,0:T(8,128)} copy(f32[1152,1536]{0,1:T(8,128)} %bitcast.98) | data formatting | bytes 14155776 | tf_op jit(solution)/shard_map/reshape | solution.py:114
  249.3 6.1 %fusion.125 = (f32[1152]{0:T(1024)S(1)}, f32[1152,1536]{1,0:T(8,128)S(1)}) fusion(f32[1152,1536]{1,0:T(8,128)} %copy.131, f32[]{:T(128)} %bitcast.97, pred[1536]{0:T(1024)(128)(4,1)S(1)} %broadcast_in_dim.162, f32[1152,2688]{1,0:T(8,128)} %convolution_multiply_fusion.2), kind=kLoop, calls=%fused_computation.124.clone.1 | loop fusion | flops 7076736 | bytes 21239812 | tf_op jit(solution)/shard_map/while/body/eval_jaxpr/reduce_max | solution.py:23
  260.7 4.4 %fusion.127 = f32[5,1152,128]{2,1,0:T(8,128)} fusion(f32[5,1152,128]{2,1,0:T(8,128)} %get-tuple-element.228, s32[]{:T(128)} %get-tuple-element.227, f32[1152,1536]{1,0:T(8,128)S(1)} %get-tuple-element.211, f32[1152,1152]{1,0:T(8,128)S(1)} %get-tuple-element.212, f32[1152]{0:T(1024)S(1)} %reduce_max.74, ...), kind=kOutput, calls=%fused_computation.11.clone.1 | convolution fusion | flops 802160640 | bytes 13673988 | tf_op jit(solution)/shard_map/while/body/eval_jaxpr/dot_general | solution.py:27
  267.4 7.3 %convolution_multiply_fusion.2 = f32[1152,2688]{1,0:T(8,128)} fusion(bf16[5,2688,128]{1,2,0:T(8,128)(2,1)S(1)} %get-tuple-element.243, s32[]{:T(128)S(6)} %select_n.184, bf16[5,1152,128]{1,2,0:T(8,128)(2,1)} %get-tuple-element.242), kind=kOutput, calls=%fused_computation.2.clone.1 | convolution fusion | flops 795820032 | bytes 13370368 | tf_op jit(solution)/shard_map/while/body/eval_jaxpr/dot_general | solution.py:129
  279.5 8.0 %copy.131 = f32[1152,1536]{1,0:T(8,128)} copy(f32[1152,1536]{0,1:T(8,128)} %bitcast.98) | data formatting | bytes 14155776 | tf_op jit(solution)/shard_map/reshape | solution.py:114
  287.7 6.1 %fusion.125 = (f32[1152]{0:T(1024)S(1)}, f32[1152,1536]{1,0:T(8,128)S(1)}) fusion(f32[1152,1536]{1,0:T(8,128)} %copy.131, f32[]{:T(128)} %bitcast.97, pred[1536]{0:T(1024)(128)(4,1)S(1)} %broadcast_in_dim.162, f32[1152,2688]{1,0:T(8,128)} %convolution_multiply_fusion.2), kind=kLoop, calls=%fused_computation.124.clone.1 | loop fusion | flops 7076736 | bytes 21239812 | tf_op jit(solution)/shard_map/while/body/eval_jaxpr/reduce_max | solution.py:23
  299.1 4.4 %fusion.127 = f32[5,1152,128]{2,1,0:T(8,128)} fusion(f32[5,1152,128]{2,1,0:T(8,128)} %get-tuple-element.228, s32[]{:T(128)} %get-tuple-element.227, f32[1152,1536]{1,0:T(8,128)S(1)} %get-tuple-element.211, f32[1152,1152]{1,0:T(8,128)S(1)} %get-tuple-element.212, f32[1152]{0:T(1024)S(1)} %reduce_max.74, ...), kind=kOutput, calls=%fused_computation.11.clone.1 | convolution fusion | flops 802160640 | bytes 13673988 | tf_op jit(solution)/shard_map/while/body/eval_jaxpr/dot_general | solution.py:27
  305.8 7.3 %convolution_multiply_fusion.2 = f32[1152,2688]{1,0:T(8,128)} fusion(bf16[5,2688,128]{1,2,0:T(8,128)(2,1)S(1)} %get-tuple-element.243, s32[]{:T(128)S(6)} %select_n.184, bf16[5,1152,128]{1,2,0:T(8,128)(2,1)} %get-tuple-element.242), kind=kOutput, calls=%fused_computation.2.clone.1 | convolution fusion | flops 795820032 | bytes 13370368 | tf_op jit(solution)/shard_map/while/body/eval_jaxpr/dot_general | solution.py:129
  317.9 8.0 %copy.131 = f32[1152,1536]{1,0:T(8,128)} copy(f32[1152,1536]{0,1:T(8,128)} %bitcast.98) | data formatting | bytes 14155776 | tf_op jit(solution)/shard_map/reshape | solution.py:114
  326.0 6.1 %fusion.125 = (f32[1152]{0:T(1024)S(1)}, f32[1152,1536]{1,0:T(8,128)S(1)}) fusion(f32[1152,1536]{1,0:T(8,128)} %copy.131, f32[]{:T(128)} %bitcast.97, pred[1536]{0:T(1024)(128)(4,1)S(1)} %broadcast_in_dim.162, f32[1152,2688]{1,0:T(8,128)} %convolution_multiply_fusion.2), kind=kLoop, calls=%fused_computation.124.clone.1 | loop fusion | flops 7076736 | bytes 21239812 | tf_op jit(solution)/shard_map/while/body/eval_jaxpr/reduce_max | solution.py:23
  337.5 4.4 %fusion.127 = f32[5,1152,128]{2,1,0:T(8,128)} fusion(f32[5,1152,128]{2,1,0:T(8,128)} %get-tuple-element.228, s32[]{:T(128)} %get-tuple-element.227, f32[1152,1536]{1,0:T(8,128)S(1)} %get-tuple-element.211, f32[1152,1152]{1,0:T(8,128)S(1)} %get-tuple-element.212, f32[1152]{0:T(1024)S(1)} %reduce_max.74, ...), kind=kOutput, calls=%fused_computation.11.clone.1 | convolution fusion | flops 802160640 | bytes 13673988 | tf_op jit(solution)/shard_map/while/body/eval_jaxpr/dot_general | solution.py:27
  344.2 7.3 %convolution_multiply_fusion.2 = f32[1152,2688]{1,0:T(8,128)} fusion(bf16[5,2688,128]{1,2,0:T(8,128)(2,1)S(1)} %get-tuple-element.243, s32[]{:T(128)S(6)} %select_n.184, bf16[5,1152,128]{1,2,0:T(8,128)(2,1)} %get-tuple-element.242), kind=kOutput, calls=%fused_computation.2.clone.1 | convolution fusion | flops 795820032 | bytes 13370368 | tf_op jit(solution)/shard_map/while/body/eval_jaxpr/dot_general | solution.py:129
  356.2 8.0 %copy.131 = f32[1152,1536]{1,0:T(8,128)} copy(f32[1152,1536]{0,1:T(8,128)} %bitcast.98) | data formatting | bytes 14155776 | tf_op jit(solution)/shard_map/reshape | solution.py:114
  364.4 6.1 %fusion.125 = (f32[1152]{0:T(1024)S(1)}, f32[1152,1536]{1,0:T(8,128)S(1)}) fusion(f32[1152,1536]{1,0:T(8,128)} %copy.131, f32[]{:T(128)} %bitcast.97, pred[1536]{0:T(1024)(128)(4,1)S(1)} %broadcast_in_dim.162, f32[1152,2688]{1,0:T(8,128)} %convolution_multiply_fusion.2), kind=kLoop, calls=%fused_computation.124.clone.1 | loop fusion | flops 7076736 | bytes 21239812 | tf_op jit(solution)/shard_map/while/body/eval_jaxpr/reduce_max | solution.py:23
  375.9 4.4 %fusion.127 = f32[5,1152,128]{2,1,0:T(8,128)} fusion(f32[5,1152,128]{2,1,0:T(8,128)} %get-tuple-element.228, s32[]{:T(128)} %get-tuple-element.227, f32[1152,1536]{1,0:T(8,128)S(1)} %get-tuple-element.211, f32[1152,1152]{1,0:T(8,128)S(1)} %get-tuple-element.212, f32[1152]{0:T(1024)S(1)} %reduce_max.74, ...), kind=kOutput, calls=%fused_computation.11.clone.1 | convolution fusion | flops 802160640 | bytes 13673988 | tf_op jit(solution)/shard_map/while/body/eval_jaxpr/dot_general | solution.py:27
  (161 shorter events, 94.8 us)
Async XLA Ops:
  6.5 5.8 %copy-start.8 = (bf16[1,1152,640]{2,1,0:T(8,128)(2,1)S(1)}, bf16[1,1152,640]{2,1,0:T(8,128)(2,1)}, u32[]{:S(2)}) copy-start(bf16[1,1152,640]{2,1,0:T(8,128)(2,1)} %param.9) | copy-start | bytes 4423684
  6.5 87.6 %all-gather.3.cloned.1.call-start = ((), (), s32[]{:S(2)}) async-start(), calls=%async_computation | async-start | bytes 8110080 | tf_op jit(solution)/shard_map/all_gather | solution.py:93
  9.4 4.3 %copy-start.7 = (bf16[1,1152,640]{2,1,0:T(8,128)(2,1)S(1)}, bf16[1,1152,640]{2,1,0:T(8,128)(2,1)}, u32[]{:S(2)}) copy-start(bf16[1,1152,640]{2,1,0:T(8,128)(2,1)} %param.8) | copy-start | bytes 4423684
  12.2 155.4 %all-gather.5.cloned.1.call-start = ((), (), s32[]{:S(2)}) async-start(), calls=%async_computation.1 | async-start | bytes 8110080 | tf_op jit(solution)/shard_map/all_gather | solution.py:94
  14.6 9.5 %copy-start.3 = (bf16[1,1152,640]{1,2,0:T(8,128)(2,1)}, bf16[1,1152,640]{1,2,0:T(8,128)(2,1)S(1)}, u32[]{:S(2)}) copy-start(bf16[1,1152,640]{1,2,0:T(8,128)(2,1)S(1)} %copy.72) | copy-start | bytes 4423684
  15.8 23.0 %collective-permute-start = (bf16[384,640]{0,1:T(8,128)(2,1)}, bf16[384,640]{0,1:T(8,128)(2,1)}, u32[]{:S(2)}, u32[]{:S(2)}) collective-permute-start(bf16[384,640]{0,1:T(8,128)(2,1)} %get-tuple-element.137), channel_id=1, source_target_pairs={{0,8},{8,16},{16,24},{24,32},{32,40},{40,48},{48,56},{56,64},{64,7... | collective-permute-start | bytes 1474568 | tf_op jit(solution)/shard_map/ppermute | solution.py:19
  22.9 15.2 %copy-start.4 = (bf16[1,1152,640]{1,2,0:T(8,128)(2,1)}, bf16[1,1152,640]{1,2,0:T(8,128)(2,1)S(1)}, u32[]{:S(2)}) copy-start(bf16[1,1152,640]{1,2,0:T(8,128)(2,1)S(1)} %copy.79) | copy-start | bytes 4423684
  22.9 11.1 %copy-start.19 = (s32[32]{0:T(128)S(1)}, s32[32]{0:T(128)}, u32[]{:S(2)}) copy-start(s32[32]{0:T(128)} %param.11) | copy-start | bytes 388
  24.1 357.4 %collective-permute-start.1 = (bf16[384,640]{0,1:T(8,128)(2,1)}, bf16[384,640]{0,1:T(8,128)(2,1)}, u32[]{:S(2)}, u32[]{:S(2)}) collective-permute-start(bf16[384,640]{0,1:T(8,128)(2,1)} %get-tuple-element.141), channel_id=1, source_target_pairs={{0,8},{8,16},{16,24},{24,32},{32,40},{40,48},{48,56},{56,64},{64,7... | collective-permute-start | bytes 1474568 | tf_op jit(solution)/shard_map/ppermute | solution.py:19
  26.0 16.3 %collective-permute-start.2 = (bf16[384,640]{0,1:T(8,128)(2,1)}, bf16[384,640]{0,1:T(8,128)(2,1)}, u32[]{:S(2)}, u32[]{:S(2)}) collective-permute-start(bf16[384,640]{0,1:T(8,128)(2,1)} %get-tuple-element.138), channel_id=1, source_target_pairs={{8,0},{16,8},{24,16},{32,24},{40,32},{48,40},{56,48},{64,56},{72,6... | collective-permute-start | bytes 1474568 | tf_op jit(solution)/shard_map/ppermute | solution.py:19
  29.3 355.8 %collective-permute-start.3 = (bf16[384,640]{0,1:T(8,128)(2,1)}, bf16[384,640]{0,1:T(8,128)(2,1)}, u32[]{:S(2)}, u32[]{:S(2)}) collective-permute-start(bf16[384,640]{0,1:T(8,128)(2,1)} %get-tuple-element.142), channel_id=1, source_target_pairs={{8,0},{16,8},{24,16},{32,24},{40,32},{48,40},{56,48},{64,56},{72,6... | collective-permute-start | bytes 1474568 | tf_op jit(solution)/shard_map/ppermute | solution.py:19
  34.0 6.6 %copy-start.6 = (bf16[1,1152,640]{1,2,0:T(8,128)(2,1)}, bf16[1,1152,640]{1,2,0:T(8,128)(2,1)S(1)}, u32[]{:S(2)}) copy-start(bf16[1,1152,640]{1,2,0:T(8,128)(2,1)S(1)} %copy.71) | copy-start | bytes 4423684
  44.1 50.1 %copy-start.12 = (f32[5,384]{1,0:T(8,128)}, f32[5,384]{1,0:T(8,128)S(1)}, u32[]{:S(2)}) copy-start(f32[5,384]{1,0:T(8,128)S(1)} %get-tuple-element.144) | copy-start | bytes 23044
  188.4 193.2 %copy-start.11 = (f32[5,384]{1,0:T(8,128)S(1)}, f32[5,384]{1,0:T(8,128)}, u32[]{:S(2)}) copy-start(f32[5,384]{1,0:T(8,128)} %copy-done.10) | copy-start | bytes 23044
  188.4 193.2 %copy-start.14 = (f32[5,384]{1,0:T(8,128)S(1)}, f32[5,384]{1,0:T(8,128)}, u32[]{:S(2)}) copy-start(f32[5,384]{1,0:T(8,128)} %fusion.31) | copy-start | bytes 23044
  188.4 193.2 %copy-start.18 = (f32[384]{0:T(512)S(1)}, f32[384]{0:T(512)}, u32[]{:S(2)}) copy-start(f32[384]{0:T(512)} %get-tuple-element.150) | copy-start | bytes 4612
  188.4 9.6 %copy-start.22 = (s32[5]{0:T(128)}, s32[5]{0:T(128)S(1)}, u32[]{:S(2)}) copy-start(s32[5]{0:T(128)S(1)} %get-tuple-element.241) | copy-start | bytes 64 | tf_op jit(solution)/shard_map/while
  222.3 4.4 %copy-start.21 = (f32[5]{0:T(128)S(1)}, f32[5]{0:T(128)}, u32[]{:S(2)}) copy-start(f32[5]{0:T(128)} %get-tuple-element.271) | copy-start | bytes 64 | tf_op jit(solution)/shard_map/while
  222.3 4.4 %copy-start.23 = (s32[5]{0:T(128)S(1)}, s32[5]{0:T(128)}, u32[]{:S(2)}) copy-start(s32[5]{0:T(128)} %copy-done.22) | copy-start | bytes 64 | tf_op jit(solution)/shard_map/while
  226.8 9.6 %copy-start.22 = (s32[5]{0:T(128)}, s32[5]{0:T(128)S(1)}, u32[]{:S(2)}) copy-start(s32[5]{0:T(128)S(1)} %get-tuple-element.241) | copy-start | bytes 64 | tf_op jit(solution)/shard_map/while
  260.7 4.4 %copy-start.21 = (f32[5]{0:T(128)S(1)}, f32[5]{0:T(128)}, u32[]{:S(2)}) copy-start(f32[5]{0:T(128)} %get-tuple-element.271) | copy-start | bytes 64 | tf_op jit(solution)/shard_map/while
  260.7 4.4 %copy-start.23 = (s32[5]{0:T(128)S(1)}, s32[5]{0:T(128)}, u32[]{:S(2)}) copy-start(s32[5]{0:T(128)} %copy-done.22) | copy-start | bytes 64 | tf_op jit(solution)/shard_map/while
  265.1 9.6 %copy-start.22 = (s32[5]{0:T(128)}, s32[5]{0:T(128)S(1)}, u32[]{:S(2)}) copy-start(s32[5]{0:T(128)S(1)} %get-tuple-element.241) | copy-start | bytes 64 | tf_op jit(solution)/shard_map/while
  299.1 4.4 %copy-start.21 = (f32[5]{0:T(128)S(1)}, f32[5]{0:T(128)}, u32[]{:S(2)}) copy-start(f32[5]{0:T(128)} %get-tuple-element.271) | copy-start | bytes 64 | tf_op jit(solution)/shard_map/while
  299.1 4.4 %copy-start.23 = (s32[5]{0:T(128)S(1)}, s32[5]{0:T(128)}, u32[]{:S(2)}) copy-start(s32[5]{0:T(128)} %copy-done.22) | copy-start | bytes 64 | tf_op jit(solution)/shard_map/while
  303.5 9.6 %copy-start.22 = (s32[5]{0:T(128)}, s32[5]{0:T(128)S(1)}, u32[]{:S(2)}) copy-start(s32[5]{0:T(128)S(1)} %get-tuple-element.241) | copy-start | bytes 64 | tf_op jit(solution)/shard_map/while
  337.5 4.4 %copy-start.21 = (f32[5]{0:T(128)S(1)}, f32[5]{0:T(128)}, u32[]{:S(2)}) copy-start(f32[5]{0:T(128)} %get-tuple-element.271) | copy-start | bytes 64 | tf_op jit(solution)/shard_map/while
  337.5 4.4 %copy-start.23 = (s32[5]{0:T(128)S(1)}, s32[5]{0:T(128)}, u32[]{:S(2)}) copy-start(s32[5]{0:T(128)} %copy-done.22) | copy-start | bytes 64 | tf_op jit(solution)/shard_map/while
  341.9 9.6 %copy-start.22 = (s32[5]{0:T(128)}, s32[5]{0:T(128)S(1)}, u32[]{:S(2)}) copy-start(s32[5]{0:T(128)S(1)} %get-tuple-element.241) | copy-start | bytes 64 | tf_op jit(solution)/shard_map/while
  375.8 4.4 %copy-start.21 = (f32[5]{0:T(128)S(1)}, f32[5]{0:T(128)}, u32[]{:S(2)}) copy-start(f32[5]{0:T(128)} %get-tuple-element.271) | copy-start | bytes 64 | tf_op jit(solution)/shard_map/while
  375.9 4.4 %copy-start.23 = (s32[5]{0:T(128)S(1)}, s32[5]{0:T(128)}, u32[]{:S(2)}) copy-start(s32[5]{0:T(128)} %copy-done.22) | copy-start | bytes 64 | tf_op jit(solution)/shard_map/while
  381.6 3.5 copy-start.2
  (10 other events, 29.7 us)
Sparse Core Ops, SparseCore 0:
  12.4 81.7 all-gather.2
  96.0 71.5 all-gather.4
where the time goes:
time: 399 us; the launch traced here: 397 us
  waiting for transfers between devices  106 us (27%)
  local copies, waits for them, and re-layouts  100 us (25%)
  matrix products  85 us (21%)
  other arithmetic  69.1 us (17%)
  between operations  13.8 us (3%)
  loops' own time  12 us (3%)
  starting transfers between devices  11.8 us (3%)
    all_gather x1, waiting for transfers between devices, on_device(): lax.all_gather(pack_values, 'win', axis=0, tiled=True)  57.9 us
    all_gather x1, waiting for transfers between devices, on_device(): lax.all_gather(pack_keys, 'win', axis=0, tiled=True)  47.5 us
    reduce_max x15, other arithmetic, head_mix(): top_score = jnp.max(scores, axis=-1, keepdims=True)  45 us
    reshape x5, local copies, waits for them, and re-layouts, on_device(): jnp.repeat(jnp.abs(query_pos[:, None] - key_pos[None, :]).astype(jnp.floa...  40.2 us
    dot_general x5, matrix products, one_head(): lax.dot_general(q_one, k_one, (((1,), (1,)), ((), ())), preferred_element...  36.4 us
    dot_general x5, matrix products, head_mix(): return jnp.dot(weights, values, preferred_element_type=jnp.float32) / totals  22.1 us
    broadcast_in_dim x5, local copies, waits for them, and re-layouts, on_device(): jnp.repeat(jnp.abs(query_pos[:, None] - key_pos[None, :]).astype(jnp.floa...  17.1 us
    another operation x1, loops' own time, on_device(): blended = lax.map(one_head, jnp.arange(heads_here, dtype=jnp.int32))  12 us
  transfers between devices with their start and end apart: 6, of which 3 were waited for; matrix products, arithmetic and copies ran while one was open for 61% of the time, Pallas kernels for 0%

commit v1 on v0

v1 whole, which is shorter than its diff:
```python
import functools
import math

import jax
import jax.numpy as jnp
from jax import lax
from jax.experimental import pallas as pl
from jax.experimental.pallas import tpu as pltpu
from jax.sharding import PartitionSpec as P

HEADS = 40
HD = 128
FT = 96
WF = 12
SF = 4
ROWS = WF * FT
SH = SF * FT
CTX = 16
GROUP = 4
HERE = 5
WIDTH = HERE * HD
SCALE = math.log2(math.e) / math.sqrt(HD)
BF = jnp.bfloat16
F32 = jnp.float32
NT = (((1,), (1,)), ((), ()))
ROOM = pltpu.CompilerParams(vmem_limit_bytes=56 * 2**20)


def with_ones(values):
    return jnp.concatenate([values, jnp.ones((values.shape[0], HD), BF)], axis=1)


def mix(scores, values_ones):
    top = jnp.max(scores, axis=-1, keepdims=True)
    weights = jnp.exp2(scores - top).astype(BF)
    return jnp.dot(weights, values_ones, preferred_element_type=F32), top


def scored(queries, keys):
    return lax.dot_general(queries, keys, NT, preferred_element_type=F32) * SCALE


def share(side, frame):
    return (frame + 1.0) / (SF + 1.0) if side == 0 else (SF - frame) / (SF + 1.0)


def own_kernel(q_ref, k_ref, v_ref, out_ref, lse_ref, *, tile):
    values_ones = with_ones(v_ref[...])
    for i in range(ROWS // tile):
        rows = slice(i * tile, (i + 1) * tile)
        mixed, top = mix(scored(q_ref[rows], k_ref[...]), values_ones)
        total = mixed[:, HD:]
        out_ref[rows] = mixed[:, :HD] / total
        lse_ref[rows] = top + jnp.log2(total)


def own_attention(queries, keys, values):
    block = pl.BlockSpec((ROWS, HD), lambda h: (0, h))
    return pl.pallas_call(
        functools.partial(own_kernel, tile=384),
        grid=(HERE,),
        in_specs=[block] * 3,
        out_specs=[block] * 2,
        out_shape=[jax.ShapeDtypeStruct((ROWS, WIDTH), F32)] * 2,
        cost_estimate=pl.CostEstimate(
            flops=HERE * ROWS * ROWS * HD * 4,
            bytes_accessed=10 * 2**20,
            transcendentals=HERE * ROWS * ROWS,
        ),
        compiler_params=ROOM,
        name="own",
    )(queries, keys, values)


def cross_kernel(edge, q_ref, left_ref, right_ref, out_ref, *, tile):
    for side in range(2):
        both = (left_ref, right_ref)[side]
        values_ones = with_ones(both[SH:])
        live = (edge[side] > 0).astype(F32)
        for i in range(SH // tile):
            start = side * (ROWS - SH) + i * tile
            mixed, _ = mix(scored(q_ref[start : start + tile], both[:SH]), values_ones)
            crossed = mixed[:, :HD] / mixed[:, HD:]
            for f in range(tile // FT):
                j = i * (tile // FT) + f
                out_ref[side * SH + j * FT : side * SH + (j + 1) * FT] = crossed[
                    f * FT : (f + 1) * FT
                ] * (live * (1.0 - share(side, j)))


def cross_attention(edge, queries, left, right):
    q_block = pl.BlockSpec((ROWS, HD), lambda h, e: (0, h))
    block = pl.BlockSpec((2 * SH, HD), lambda h, e: (0, h))
    return pl.pallas_call(
        functools.partial(cross_kernel, tile=384),
        grid_spec=pltpu.PrefetchScalarGridSpec(
            num_scalar_prefetch=1,
            grid=(HERE,),
            in_specs=[q_block, block, block],
            out_specs=block,
        ),
        out_shape=jax.ShapeDtypeStruct((2 * SH, WIDTH), F32),
        cost_estimate=pl.CostEstimate(
            flops=HERE * 2 * SH * SH * HD * 4,
            bytes_accessed=7 * 2**20,
            transcendentals=HERE * 2 * SH * SH,
        ),
        compiler_params=ROOM,
        name="cross",
    )(edge, queries, left, right)


def context_kernel(
    place, edge, slope_ref, far_ref, q_ref, own_ref, lse_ref, cross_ref, frames_ref, out_ref,
    keys, values, sem, *, tile
):
    head = pl.program_id(0)
    used = edge[2]

    def copies(slot, h):
        lanes = pl.ds(pl.multiple_of(h * HD, HD), HD)
        rows = pl.ds(slot * FT, FT)
        window, which = place[slot], place[slot + CTX]
        return (
            pltpu.make_async_copy(
                frames_ref.at[window, which, :, lanes], keys.at[h, rows], sem.at[h]
            ),
            pltpu.make_async_copy(
                frames_ref.at[window, which + 2, :, lanes], values.at[h, rows], sem.at[h]
            ),
        )

    @pl.when(head == 0)
    def _():
        for h in range(HERE):
            for slot in range(CTX):

                @pl.when(slot < used)
                def _():
                    for copy in copies(slot, h):
                        copy.start()

                @pl.when(slot >= used)
                def _():
                    keys[h, slot * FT : (slot + 1) * FT] = jnp.zeros((FT, HD), BF)
                    values[h, slot * FT : (slot + 1) * FT] = jnp.zeros((FT, HD), BF)

    for slot in range(CTX):

        @pl.when(slot < used)
        def _():
            for copy in copies(slot, head):
                copy.wait()

    slope = slope_ref[head]
    per_tile = tile // FT

    def work(groups):
        width = groups * GROUP * FT
        k = keys[head, :width]
        values_ones = with_ones(values[head, :width])
        for i in range(ROWS // tile):
            rows = slice(i * tile, (i + 1) * tile)
            scores = scored(q_ref[rows], k)
            parts = [
                scores[f * FT : (f + 1) * FT]
                + far_ref[i * per_tile + f : i * per_tile + f + 1, :width] * slope
                for f in range(per_tile)
            ]
            mixed, top = mix(jnp.concatenate(parts, axis=0), values_ones)
            lse = lse_ref[rows]
            higher = jnp.maximum(lse, top)
            of_own = jnp.exp2(lse - higher)
            of_context = jnp.exp2(top - higher)
            out = (own_ref[rows] * of_own + mixed[:, :HD] * of_context) / (
                of_own + mixed[:, HD:] * of_context
            )
            for f in range(per_tile):
                j = i * per_tile + f
                piece = out[f * FT : (f + 1) * FT]
                side = 0 if j < SF else 1
                if j < SF or j >= WF - SF:
                    j_in = j if j < SF else j - (WF - SF)
                    live = (edge[side] > 0).astype(F32)
                    at = side * SH + j_in * FT
                    piece = piece * (1.0 - live * (1.0 - share(side, j_in)))
                    piece = piece + cross_ref[at : at + FT]
                out_ref[j * FT : (j + 1) * FT] = piece.astype(BF)

    for groups in range(1, CTX // GROUP + 1):

        @pl.when((used + GROUP - 1) // GROUP == groups)
        def _():
            work(groups)


def context_attention(place, edge, slopes, far, queries, own, lse, crossed, frames):
    block = pl.BlockSpec((ROWS, HD), lambda h, *_: (0, h))
    return pl.pallas_call(
        functools.partial(context_kernel, tile=192),
        grid_spec=pltpu.PrefetchScalarGridSpec(
            num_scalar_prefetch=3,
            grid=(HERE,),
            in_specs=[
                pl.BlockSpec((WF, CTX * FT), lambda h, *_: (0, 0)),
                block,
                block,
                block,
                pl.BlockSpec((2 * SH, HD), lambda h, *_: (0, h)),
                pl.BlockSpec(memory_space=pl.ANY),
            ],
            out_specs=block,
            scratch_shapes=[
                pltpu.VMEM((HERE, CTX * FT, HD), BF),
                pltpu.VMEM((HERE, CTX * FT, HD), BF),
                pltpu.SemaphoreType.DMA((HERE,)),
            ],
        ),
        out_shape=jax.ShapeDtypeStruct((ROWS, WIDTH), BF),
        cost_estimate=pl.CostEstimate(
            flops=HERE * ROWS * CTX * FT * HD * 4,
            bytes_accessed=14 * 2**20,
            transcendentals=HERE * ROWS * CTX * FT,
        ),
        compiler_params=ROOM,
        name="context",
    )(place, edge, slopes, far, queries, own, lse, crossed, frames)


def shifted(value, by):
    peers = lax.axis_size("win")
    pairs = [(i, i + by) for i in range(peers) if 0 <= i + by < peers]
    return lax.ppermute(value, "win", pairs)


def named_frames(context_index, win_id):
    asked = (context_index >= 0) & (context_index // WF == win_id)
    frame = context_index % WF
    low = jnp.min(jnp.where(asked, frame, WF))
    high = jnp.max(jnp.where(asked, frame, -1))
    return jnp.clip(low, 0, WF - 1), jnp.clip(high, 0, WF - 1)


def my_slots(context_index, window_start, win_id):
    windows = context_index.shape[0]
    entries = lax.dynamic_index_in_dim(context_index, win_id, 0, keepdims=False)
    live = entries >= 0
    at = jnp.cumsum(live.astype(jnp.int32)) - 1
    move = live[None, :] & (at[None, :] == jnp.arange(CTX, dtype=jnp.int32)[:, None])
    entries = jnp.sum(jnp.where(move, entries[None, :], 0), axis=1)
    used = jnp.sum(live.astype(jnp.int32))
    live = jnp.arange(CTX, dtype=jnp.int32) < used
    source = entries // WF
    frame = entries % WF
    names = (context_index >= 0)[None] & (context_index[None] // WF == source[:, None, None])
    low = jnp.min(jnp.where(names, context_index[None] % WF, WF), axis=(1, 2))
    which = (frame != low).astype(jnp.int32)
    from_table = source[:, None] == jnp.arange(windows, dtype=jnp.int32)[None, :]
    key_pos = jnp.sum(jnp.where(from_table, window_start[None, :], 0), axis=1) + frame
    my_start = lax.dynamic_index_in_dim(window_start, win_id, 0, keepdims=False)
    query_pos = my_start + jnp.arange(WF, dtype=jnp.int32)
    distance = jnp.abs(query_pos[:, None] - key_pos[None, :]).astype(F32)
    far = jnp.where(live[None, :], -distance, -1e30)
    far = jnp.broadcast_to(far[:, :, None], (WF, CTX, FT)).reshape(WF, CTX * FT)
    return jnp.concatenate([source, which]), used, far


def on_device(query_tokens, key_tokens, value_tokens, context_index, window_start):
    queries, keys, values = query_tokens[0], key_tokens[0], value_tokens[0]
    windows = lax.axis_size("win")
    win_id = lax.axis_index("win")
    low, high = named_frames(context_index, win_id)
    packed = jnp.concatenate(
        [
            lax.dynamic_slice_in_dim(array, frame * FT, FT, 0)
            for array in (keys, values)
            for frame in (low, high)
        ],
        axis=0,
    )
    frames = lax.all_gather(packed, "win", axis=0, tiled=True)
    frames = frames.reshape(windows, 4, FT, WIDTH)
    left = shifted(jnp.concatenate([keys[ROWS - SH :], values[ROWS - SH :]], axis=0), 1)
    right = shifted(jnp.concatenate([keys[:SH], values[:SH]], axis=0), -1)
    place, used, far = my_slots(context_index, window_start, win_id)
    edge = jnp.stack([win_id, windows - 1 - win_id, used]).astype(jnp.int32)
    head_ids = lax.axis_index("head") * HERE + jnp.arange(HERE, dtype=jnp.int32)
    slopes = 0.25 * math.log2(math.e) * jnp.exp2(-8.0 * head_ids.astype(F32) / HEADS)
    own, lse = own_attention(queries, keys, values)
    crossed = cross_attention(edge, queries, left, right)
    return context_attention(place, edge, slopes, far, queries, own, lse, crossed, frames)[None]


def solution(mesh):
    spec = P("win", None, "head")
    return jax.shard_map(
        on_device, mesh=mesh, in_specs=(spec, spec, spec, P(), P()), out_specs=spec, check_vma=False
    )
```

time: 399 us -> 147 us (0.37)
  local copies, waits for them, and re-layouts: 100 us -> 5.11 us
  matrix products: 85 us -> 0 us
  other arithmetic: 69.1 us -> 8.79 us
  Pallas kernels: 0 us -> 41.5 us
  waiting for transfers between devices: 106 us -> 68.4 us
  loops' own time: 12 us -> 0 us
  starting transfers between devices: 11.8 us -> 6.5 us
    dot_general x18 -> x0, matrix products: 85 us -> none  [the longest x5 36.4 us: one_head(): lax.dot_general(q_one, k_one, (((1,), (1,)), ((), ())), preferred_element...]
    reduce_max x15 -> x0, other arithmetic: 45 us -> none  [head_mix(): top_score = jnp.max(scores, axis=-1, keepdims=True)]
    all_gather x2 -> x1, waiting for transfers between devices: 105 us -> 61.8 us  [on_device(): frames = lax.all_gather(packed, 'win', axis=0, tiled=True)]
    pallas_call x0 -> x3, Pallas kernels: none -> 41.5 us  [the longest x1 17.9 us: context_attention(): pl.pallas_call(functools.partial(context_kernel, tile=192), grid_spec=plt...]
    reshape x5 -> x1, local copies, waits for them, and re-layouts: 40.2 us -> 0.76 us  [my_slots(): far = jnp.broadcast_to(far[:, :, None], (WF, CTX, FT)).reshape(WF, CTX * FT)]
    broadcast_in_dim x15 -> x1, local copies, waits for them, and re-layouts: 17.9 us -> 0.08 us  [my_slots(): far = jnp.broadcast_to(far[:, :, None], (WF, CTX, FT)).reshape(WF, CTX * FT)]
    reduce_sum x8 -> x3, other arithmetic: 14.8 us -> 1.01 us  [the longest x1 0.71 us: my_slots(): used = jnp.sum(live.astype(jnp.int32))]
    another operation x1 -> x0, loops' own time: 12 us -> none  [on_device(): blended = lax.map(one_head, jnp.arange(heads_here, dtype=jnp.int32))]
  transfers between devices with their start and end apart: 6 -> 3, of which waited for: 3 -> 2; matrix products, arithmetic and copies ran while one was open for 61% -> 6% of each run, Pallas kernels for 0% -> 16%
where the time goes in v1:
time: 147 us; the launch traced here: 145 us
  waiting for transfers between devices  68.4 us (47%)
  Pallas kernels  41.5 us (28%)
  between operations  14.8 us (10%)
  other arithmetic  8.79 us (6%)
  starting transfers between devices  6.5 us (4%)
  local copies, waits for them, and re-layouts  5.11 us (3%)
    all_gather x1, waiting for transfers between devices, on_device(): frames = lax.all_gather(packed, 'win', axis=0, tiled=True)  61.8 us
    pallas_call x1, Pallas kernels, context_attention(): pl.pallas_call(functools.partial(context_kernel, tile=192), grid_spec=plt...  17.9 us
    pallas_call x1, Pallas kernels, own_attention(): pl.pallas_call(functools.partial(own_kernel, tile=384), grid=(HERE,), in_...  16.1 us
    pallas_call x1, Pallas kernels, cross_attention(): pl.pallas_call(functools.partial(cross_kernel, tile=384), grid_spec=pltpu...  7.47 us
    ppermute x2, waiting for transfers between devices, shifted(): return lax.ppermute(value, 'win', pairs)  6.62 us
    ppermute x2, starting transfers between devices, shifted(): return lax.ppermute(value, 'win', pairs)  6.5 us
  transfers between devices with their start and end apart: 3, of which 2 were waited for; matrix products, arithmetic and copies ran while one was open for 6% of the time, Pallas kernels for 16%

profile of v1, /device:TPU:1, one launch (start us, length us, event | category | flops | bytes accessed | tf_op | source)
XLA Modules:
  0.0 145.2 jit_solution(16455078848811676555)
XLA Ops:
  6.5 0.8 compare_and_fusion
  7.4 1.4 select_reduce_fusion.2
  10.1 1.1 dynamic-slice_bitcast_fusion.1
  11.2 0.8 pad_maximum_fusion.2
  12.0 0.0 all-gather.2.cloned.1.call-update
  12.1 1.4 slice_bitcast_fusion
  13.4 0.1 pad_maximum_fusion
  13.5 4.5 %collective-permute-start = (bf16[768,640]{1,0:T(8,128)(2,1)S(1)}, bf16[768,640]{1,0:T(8,128)(2,1)S(1)}, u32[]{:S(2)}, u32[]{:S(2)}) collective-permute-start(bf16[768,640]{1,0:T(8,128)(2,1)S(1)} %pad_maximum_fusion), channel_id=1, source_target_pairs={{0,8},{8,16},{16,24},{24,32},{32,40},{40,48},{48,56},{56,64},{64,7... | collective-permute-start | bytes 2949128 | tf_op jit(solution)/shard_map/ppermute | solution.py:233
  18.0 0.1 pad_maximum_fusion.1
  18.1 2.0 %collective-permute-start.1 = (bf16[768,640]{1,0:T(8,128)(2,1)S(1)}, bf16[768,640]{1,0:T(8,128)(2,1)}, u32[]{:S(2)}, u32[]{:S(2)}) collective-permute-start(bf16[768,640]{1,0:T(8,128)(2,1)S(1)} %pad_maximum_fusion.1), channel_id=1, source_target_pairs={{8,0},{16,8},{24,16},{32,24},{40,32},{48,40},{56,48},{64,56},{72,6... | collective-permute-start | bytes 2949128 | tf_op jit(solution)/shard_map/ppermute | solution.py:233
  20.2 0.7 dynamic_slice.29
  20.8 0.2 fusion.4
  21.0 0.2 dynamic-slice_reduce_fusion
  21.2 0.6 iota_add_fusion
  21.9 0.1 add_reduce_fusion
  22.0 0.1 select_reduce_fusion.4
  22.1 0.2 select_reduce_fusion.3
  22.3 0.7 fusion.2
  23.0 0.6 iota_compare_fusion.2
  23.7 0.1 negate_select_fusion
  23.7 0.1 broadcast_in_dim.85
  23.8 0.8 reshape.146.far_ref
  24.6 0.5 exponential_multiply_fusion.slope_ref
  25.1 0.5 select_reduce_fusion
  25.6 0.6 pad_add_fusion.place
  26.2 1.2 pad_add_fusion.1.edge
  27.4 16.1 %own.1 = (f32[1152,640]{1,0:T(8,128)}, f32[1152,640]{1,0:T(8,128)}) custom-call(bf16[1152,640]{1,0:T(8,128)(2,1)} %bitcast.28, bf16[1152,640]{1,0:T(8,128)(2,1)} %bitcast.31, bf16[1152,640]{1,0:T(8,128)(2,1)} %bitcast.32), custom_call_target="tpu_custom_call" | custom-call | flops 3397386240 | bytes 10485760 | tf_op jit(solution)/shard_map/own/pallas_call | solution.py:59
  43.5 6.6 %collective-permute-done.left_ref = bf16[768,640]{1,0:T(8,128)(2,1)S(1)} collective-permute-done((bf16[768,640]{1,0:T(8,128)(2,1)S(1)}, bf16[768,640]{1,0:T(8,128)(2,1)S(1)}, u32[]{:S(2)}, u32[]{:S(2)}) %collective-permute-start) | collective-permute-done | bytes 983072 | tf_op jit(solution)/shard_map/ppermute | solution.py:233
  50.1 0.9 copy-done.1
  51.1 7.5 %cross.1.cross_ref = f32[768,640]{1,0:T(8,128)} custom-call(s32[3]{0:T(128)} %pad_add_fusion.1.edge, bf16[1152,640]{1,0:T(8,128)(2,1)} %bitcast.29, bf16[768,640]{1,0:T(8,128)(2,1)} %copy-done.1, bf16[768,640]{1,0:T(8,128)(2,1)} %collective-permute-done.1.right_ref), custom_call_target="tpu_custom_call" | custom-call | flops 754974720 | bytes 7340032 | tf_op jit(solution)/shard_map/cross/pallas_call | solution.py:94
  58.6 61.8 %all-gather.2.cloned.1.call-done = bf16[12288,640]{1,0:T(8,128)(2,1)} async-done(((bf16[384,640]{1,0:T(8,128)(2,1)}), bf16[12288,640]{1,0:T(8,128)(2,1)}) %all-gather.2.cloned.1.call-update) | async-done | bytes 15728656 | tf_op jit(solution)/shard_map/all_gather | solution.py:281
  120.4 17.9 %context.1 = bf16[1152,640]{1,0:T(8,128)(2,1)} custom-call(s32[32]{0:T(128)} %pad_add_fusion.place, s32[3]{0:T(128)} %pad_add_fusion.1.edge, f32[5]{0:T(128)} %exponential_multiply_fusion.slope_ref, f32[12,1536]{1,0:T(8,128)} %reshape.146.far_ref, bf16[1152,640]{1,0:T(8,128)(2,1)} %bitcast.30, f32[1152,640]{1,0:T(8,128)} %get-tuple-element.7.own_ref, ...), custom_call_target="tpu_custom_call" | custom-call | flops 4529848320 | bytes 14680064 | tf_op jit(solution)/shard_map/context/pallas_call | solution.py:199
  (13 shorter events, 0.1 us)
Async XLA Ops:
  6.5 5.5 %copy-start = (bf16[1,1152,640]{2,1,0:T(8,128)(2,1)S(1)}, bf16[1,1152,640]{2,1,0:T(8,128)(2,1)}, u32[]{:S(2)}) copy-start(bf16[1,1152,640]{2,1,0:T(8,128)(2,1)} %param.6) | copy-start | bytes 4423684
  6.5 113.8 %all-gather.2.cloned.1.call-start = ((), (), s32[]{:S(2)}) async-start(), calls=%async_computation | async-start | bytes 16220160 | tf_op jit(solution)/shard_map/all_gather | solution.py:281
  13.4 6.7 %copy-start.3 = (s32[32]{0:T(128)S(1)}, s32[32]{0:T(128)}, u32[]{:S(2)}) copy-start(s32[32]{0:T(128)} %param.9) | copy-start | bytes 388
  13.4 7.4 %copy-start.2 = (s32[32,16]{0,1:T(8,128)S(1)}, s32[32,16]{0,1:T(8,128)}, u32[]{:S(2)}) copy-start(s32[32,16]{0,1:T(8,128)} %param.8) | copy-start | bytes 6148
  13.5 36.6 %collective-permute-start = (bf16[768,640]{1,0:T(8,128)(2,1)S(1)}, bf16[768,640]{1,0:T(8,128)(2,1)S(1)}, u32[]{:S(2)}, u32[]{:S(2)}) collective-permute-start(bf16[768,640]{1,0:T(8,128)(2,1)S(1)} %pad_maximum_fusion), channel_id=1, source_target_pairs={{0,8},{8,16},{16,24},{24,32},{32,40},{40,48},{48,56},{56,64},{64,7... | collective-permute-start | bytes 2949128 | tf_op jit(solution)/shard_map/ppermute | solution.py:233
  18.1 32.0 %collective-permute-start.1 = (bf16[768,640]{1,0:T(8,128)(2,1)S(1)}, bf16[768,640]{1,0:T(8,128)(2,1)}, u32[]{:S(2)}, u32[]{:S(2)}) collective-permute-start(bf16[768,640]{1,0:T(8,128)(2,1)S(1)} %pad_maximum_fusion.1), channel_id=1, source_target_pairs={{8,0},{16,8},{24,16},{32,24},{40,32},{48,40},{56,48},{64,56},{72,6... | collective-permute-start | bytes 2949128 | tf_op jit(solution)/shard_map/ppermute | solution.py:233
  50.1 0.9 copy-start.1
Sparse Core Ops, SparseCore 0:
  12.2 108.1 all-gather.1

commit v2 on v1

v2 whole, which is shorter than its diff:
```python
import functools
import math

import jax
import jax.numpy as jnp
from jax import lax
from jax.experimental import pallas as pl
from jax.experimental.pallas import tpu as pltpu
from jax.sharding import PartitionSpec as P

HEADS = 40
HD = 128
FT = 96
WF = 12
SF = 4
ROWS = WF * FT
SH = SF * FT
CTX = 16
WINDOWS = 32
PLANES = 8
LANES = 128
LOW, START, WIN, HEAD = CTX, 2 * CTX, 2 * CTX + WINDOWS, 2 * CTX + WINDOWS + 1
HERE = 5
WIDTH = HERE * HD
SCALE = math.log2(math.e) / math.sqrt(HD)
BF = jnp.bfloat16
F32 = jnp.float32
NT = (((1,), (1,)), ((), ()))
ROOM = pltpu.CompilerParams(vmem_limit_bytes=56 * 2**20)


def placed(win):
    return win >> 2, win >> 1 & 1, win & 1


def lasting(microseconds):
    return pl.CostEstimate(flops=int(microseconds * 2e7), bytes_accessed=0, transcendentals=0)


def with_ones(values):
    return jnp.concatenate([values, jnp.ones((values.shape[0], HD), BF)], axis=1)


def mix(scores, values_ones):
    top = jnp.max(scores, axis=-1, keepdims=True)
    weights = jnp.exp2(scores - top).astype(BF)
    return jnp.dot(weights, values_ones, preferred_element_type=F32), top


def scored(queries, keys):
    return lax.dot_general(queries, keys, NT, preferred_element_type=F32) * SCALE


def share(side, frame):
    return (frame + 1.0) / (SF + 1.0) if side == 0 else (SF - frame) / (SF + 1.0)


def own_kernel(q_ref, k_ref, v_ref, out_ref, lse_ref, *, tile):
    values_ones = with_ones(v_ref[...])
    for i in range(ROWS // tile):
        rows = slice(i * tile, (i + 1) * tile)
        mixed, top = mix(scored(q_ref[rows], k_ref[...]), values_ones)
        total = mixed[:, HD:]
        out_ref[rows] = mixed[:, :HD] / total
        lse_ref[rows] = top + jnp.log2(total)


def own_attention(queries, keys, values, first, count, before=None):
    block = pl.BlockSpec((ROWS, HD), lambda h: (0, first + h))
    untouched = [] if before is None else [pl.BlockSpec(memory_space=pl.ANY)] * 2

    def kernel(q_ref, k_ref, v_ref, *refs):
        own_kernel(q_ref, k_ref, v_ref, refs[-2], refs[-1], tile=384)

    return pl.pallas_call(
        kernel,
        grid=(count,),
        in_specs=[block] * 3 + untouched,
        out_specs=[block] * 2,
        out_shape=[jax.ShapeDtypeStruct((ROWS, WIDTH), F32)] * 2,
        input_output_aliases={} if before is None else {3: 0, 4: 1},
        cost_estimate=lasting(1.0 + 3.0 * count),
        compiler_params=ROOM,
        name="own",
    )(queries, keys, values, *(() if before is None else before))


def has_side(info, side):
    return (info[WIN] != (0, WINDOWS - 1)[side]).astype(F32)


def cross_kernel(info, q_ref, left_ref, right_ref, out_ref, *, tile):
    for side in range(2):
        both = (left_ref, right_ref)[side]
        values_ones = with_ones(both[SH:])
        live = has_side(info, side)
        for i in range(SH // tile):
            start = side * (ROWS - SH) + i * tile
            mixed, _ = mix(scored(q_ref[start : start + tile], both[:SH]), values_ones)
            crossed = mixed[:, :HD] / mixed[:, HD:]
            for f in range(tile // FT):
                j = i * (tile // FT) + f
                out_ref[side * SH + j * FT : side * SH + (j + 1) * FT] = crossed[
                    f * FT : (f + 1) * FT
                ] * (live * (1.0 - share(side, j)))


def cross_attention(info, queries, left, right):
    q_block = pl.BlockSpec((ROWS, HD), lambda h, e: (0, h))
    block = pl.BlockSpec((2 * SH, HD), lambda h, e: (0, h))
    return pl.pallas_call(
        functools.partial(cross_kernel, tile=384),
        grid_spec=pltpu.PrefetchScalarGridSpec(
            num_scalar_prefetch=1,
            grid=(HERE,),
            in_specs=[q_block, block, block],
            out_specs=block,
        ),
        out_shape=jax.ShapeDtypeStruct((2 * SH, WIDTH), F32),
        cost_estimate=lasting(7.5),
        compiler_params=ROOM,
        name="cross",
    )(info, queries, left, right)


def plan(info, lists, most, wanted):
    z, x, core = placed(info[WIN])
    count = jnp.int32(0)
    for slot in range(CTX):
        entry = info[slot]
        source = jnp.maximum(entry, 0) // WF
        frame = entry - source * WF
        which = (frame != info[LOW + slot]).astype(jnp.int32)
        s_z, s_x, s_core = placed(source)
        other = (s_x != x).astype(jnp.int32)
        far_core = (s_core != core).astype(jnp.int32)
        away = (s_z - z) & (PLANES - 1)
        up = (away > 4).astype(jnp.int32)
        steps = jnp.where(up == 1, PLANES - away, away)
        swapped = jnp.where(up == 1, core, 1 - core)
        half = jnp.where(up == 1, s_core, 1 - s_core)
        array, start = wanted(source, steps, other, far_core, swapped, half)
        lists[count] = array
        lists[most + 1 + count] = start + which
        lists[2 * most + 2 + count] = info[START + source] + frame
        count = count + ((entry >= 0) & (array >= 0)).astype(jnp.int32)
    lists[3 * most + 3] = count


def everywhere(source, steps, other, far_core, swapped, half):
    at_home = jnp.where(other == 1, 1 + far_core, 0)
    array = jnp.where(steps == 4, 15 + other * 2 + far_core, 4 * steps - 1 + other * 2 + swapped)
    start = jnp.where((steps == 0) | (steps == 4), 0, half * 4)
    return jnp.where(steps == 0, at_home, array), start


def widths_of(most):
    return [w for w in range(2 * LANES, most * FT, 2 * LANES)] + [most * FT]


def context_kernel(info, q_ref, own_ref, lse_ref, *refs, tile, most, sources, wanted, last):
    cross_ref = refs[0] if last else None
    refs = refs[1:] if last else refs
    source_refs, refs = refs[:sources], refs[sources:]
    out_ref, lse_out_ref = (refs[0], None) if last else refs[:2]
    keys, values, far_ref, lists, sem = refs[-5:]
    head = pl.program_id(0)

    def copies(source, start, slot):
        rows = pl.ds(slot * FT, FT)
        k_rows = pl.ds(pl.multiple_of(start * FT, FT), FT)
        v_rows = pl.ds(pl.multiple_of((start + 2) * FT, FT), FT)
        return (
            pltpu.make_async_copy(source.at[k_rows], keys.at[rows], sem.at[0]),
            pltpu.make_async_copy(source.at[v_rows], values.at[rows], sem.at[1]),
        )

    @pl.when(head == 0)
    def _():
        plan(info, lists, most, wanted)
        used = lists[3 * most + 3]
        for slot in range(most):
            for s in range(sources):

                @pl.when((slot < used) & (lists[slot] == s))
                def _():
                    for copy in copies(source_refs[s], lists[most + 1 + slot], slot):
                        copy.start()

            @pl.when(slot >= used)
            def _():
                keys[slot * FT : (slot + 1) * FT] = jnp.zeros((FT, WIDTH), BF)
                values[slot * FT : (slot + 1) * FT] = jnp.zeros((FT, WIDTH), BF)

        lane = lax.broadcasted_iota(jnp.int32, (1, most * FT), 1)
        key_pos = jnp.zeros((1, most * FT), F32)
        for slot in range(most):
            here = jnp.where(slot < used, lists[2 * most + 2 + slot].astype(F32), 1e30)
            key_pos = jnp.where(lane >= slot * FT, here, key_pos)
        frame = lax.broadcasted_iota(jnp.int32, (WF, 1), 0)
        query_pos = (info[START + info[WIN]] + frame).astype(F32)
        far_ref[...] = -jnp.abs(query_pos - key_pos)

        for slot in range(most):

            @pl.when(slot < used)
            def _():
                for copy in copies(source_refs[0], 0, slot):
                    copy.wait()

    used = lists[3 * most + 3]
    lanes = pl.ds(pl.multiple_of(head * HD, HD), HD)
    which_head = (info[HEAD] + head).astype(F32)
    slope = jnp.exp2(jnp.full((1, LANES), -8.0 / HEADS, F32) * which_head)[:, :1]
    slope = slope * (0.25 * math.log2(math.e))
    per_tile = tile // FT

    def finish(i, out):
        for f in range(per_tile):
            j = i * per_tile + f
            piece = out[f * FT : (f + 1) * FT]
            side = 0 if j < SF else 1
            if j < SF or j >= WF - SF:
                j_in = j if j < SF else j - (WF - SF)
                at = side * SH + j_in * FT
                piece = piece * (1.0 - has_side(info, side) * (1.0 - share(side, j_in)))
                piece = piece + cross_ref[at : at + FT]
            out_ref[j * FT : (j + 1) * FT] = piece.astype(BF)

    def work(width):
        if width:
            k = keys[:width, lanes]
            values_ones = with_ones(values[:width, lanes])
        for i in range(ROWS // tile):
            rows = slice(i * tile, (i + 1) * tile)
            if not width:
                if last:
                    finish(i, own_ref[rows])
                else:
                    out_ref[rows] = own_ref[rows]
                    lse_out_ref[rows] = lse_ref[rows]
                continue
            scores = scored(q_ref[rows], k)
            parts = [
                scores[f * FT : (f + 1) * FT]
                + far_ref[i * per_tile + f : i * per_tile + f + 1, :width] * slope
                for f in range(per_tile)
            ]
            mixed, top = mix(jnp.concatenate(parts, axis=0), values_ones)
            lse = lse_ref[rows]
            higher = jnp.maximum(lse, top)
            of_own = jnp.exp2(lse - higher)
            of_context = jnp.exp2(top - higher)
            total = of_own + mixed[:, HD:] * of_context
            out = (own_ref[rows] * of_own + mixed[:, :HD] * of_context) / total
            if last:
                finish(i, out)
            else:
                out_ref[rows] = out
                lse_out_ref[rows] = higher + jnp.log2(total)

    below = 0
    for width in [0] + widths_of(most):
        fits = width // FT

        @pl.when((used <= fits) & (used >= below))
        def _():
            work(width)

        below = fits + 1


def context_attention(info, queries, state, sources, most, wanted, crossed=None):
    last = crossed is not None
    block = pl.BlockSpec((ROWS, HD), lambda h, *_: (0, h))
    cross_block = pl.BlockSpec((2 * SH, HD), lambda h, *_: (0, h))
    f32 = jax.ShapeDtypeStruct((ROWS, WIDTH), F32)
    return pl.pallas_call(
        functools.partial(
            context_kernel,
            tile=192,
            most=most,
            sources=len(sources),
            wanted=wanted,
            last=last,
        ),
        grid_spec=pltpu.PrefetchScalarGridSpec(
            num_scalar_prefetch=1,
            grid=(HERE,),
            in_specs=[block, block, block]
            + [cross_block] * last
            + [pl.BlockSpec(memory_space=pl.ANY)] * len(sources),
            out_specs=block if last else [block, block],
            scratch_shapes=[
                pltpu.VMEM((most * FT, WIDTH), BF),
                pltpu.VMEM((most * FT, WIDTH), BF),
                pltpu.VMEM((WF, most * FT), F32),
                pltpu.SMEM((3 * most + 4,), jnp.int32),
                pltpu.SemaphoreType.DMA((2,)),
            ],
        ),
        out_shape=jax.ShapeDtypeStruct((ROWS, WIDTH), BF) if last else [f32, f32],
        cost_estimate=lasting(17.0),
        compiler_params=ROOM,
        name="context",
    )(info, queries, *state, *([crossed] * last), *sources)


def moved(value, move):
    peers = lax.axis_size("win")

    def target(win):
        z, x, core = move(*placed(win))
        return z % (peers // 4) * 4 + x * 2 + core

    return lax.ppermute(value, "win", [(i, target(i)) for i in range(peers)])


def round_z(value):
    return moved(value, lambda z, x, core: (z + 1 - 2 * core, x, core))


def to_sibling(value):
    return moved(value, lambda z, x, core: (z, x, 1 - core))


def to_partner(value):
    return moved(value, lambda z, x, core: (z, 1 - x, core))


def shifted(value, by):
    peers = lax.axis_size("win")
    pairs = [(i, i + by) for i in range(peers) if 0 <= i + by < peers]
    return lax.ppermute(value, "win", pairs)


def pack_kernel(index_ref, keys_ref, values_ref, out_ref, sem):
    first = lax.axis_index("win") * WF
    entries = index_ref[...]
    asked = (entries >= first) & (entries < first + WF)
    low = jnp.min(jnp.where(asked, entries - first, WF))
    high = jnp.max(jnp.where(asked, entries - first, -1))
    copies = []
    for source in (keys_ref, values_ref):
        for frame in (low, high):
            start = pl.multiple_of(jnp.clip(frame, 0, WF - 1) * FT, FT)
            at = len(copies)
            copies.append(
                pltpu.make_async_copy(
                    source.at[pl.ds(start, FT)], out_ref.at[pl.ds(at * FT, FT)], sem.at[at]
                )
            )
    for copy in copies:
        copy.start()
    for copy in copies:
        copy.wait()


def packed(context_index, keys, values):
    anywhere = pl.BlockSpec(memory_space=pl.ANY)
    return pl.pallas_call(
        pack_kernel,
        in_specs=[pl.BlockSpec(memory_space=pltpu.VMEM), anywhere, anywhere],
        out_specs=pl.BlockSpec(memory_space=pltpu.VMEM),
        out_shape=jax.ShapeDtypeStruct((4 * FT, WIDTH), BF),
        scratch_shapes=[pltpu.SemaphoreType.DMA((4,))],
        name="pack",
    )(context_index, keys, values)


def slot_info(context_index, window_start):
    win_id = lax.axis_index("win")
    entries = lax.dynamic_index_in_dim(context_index, win_id, 0, keepdims=False)
    first = jnp.maximum(entries, 0) // WF * WF
    frame = context_index[None] - first[:, None, None]
    low = jnp.min(jnp.where((frame >= 0) & (frame < WF), frame, WF), axis=(1, 2))
    ids = jnp.stack([win_id, lax.axis_index("head") * HERE]).astype(jnp.int32)
    return jnp.concatenate([entries, low, window_start, ids])


def together(*values):
    return lax.optimization_barrier(values)


def on_device(query_tokens, key_tokens, value_tokens, context_index, window_start):
    queries, keys, values = query_tokens[0], key_tokens[0], value_tokens[0]
    mine = packed(context_index, keys, values)
    sibling = to_sibling(mine)
    partner = to_partner(mine)
    info = slot_info(context_index, window_start)
    one0 = jnp.concatenate([mine, sibling], axis=0)
    one1 = round_z(one0)
    last_rows = jnp.concatenate([keys[ROWS - SH :], values[ROWS - SH :]], axis=0)
    first_rows = jnp.concatenate([keys[:SH], values[:SH]], axis=0)
    _, first_queries, last_rows, first_rows = together(one0, queries, last_rows, first_rows)
    left, right = shifted(last_rows, 1), shifted(first_rows, -1)
    state = own_attention(first_queries, keys, values, 0, 3)
    one1, partner, *state = together(one1, partner, *state)
    one2 = round_z(one1)
    partner_sibling = to_sibling(partner)
    two0 = jnp.concatenate([partner, partner_sibling], axis=0)
    two1 = round_z(two0)
    one1_back = to_sibling(one1)
    _, *state = together(two0, *state)
    state = own_attention(queries, keys, values, 3, 2, state)
    one2, *state = together(one2, *state)
    one3 = round_z(one2)
    one2_back = to_sibling(one2)
    two2 = round_z(two1)
    two1_back = to_sibling(two1)
    one4 = round_z(one3[: 4 * FT])
    one3_back = to_sibling(one3)
    _, left, right = together(two1, left, right)
    crossed = cross_attention(info, queries, left, right)
    two2, crossed = together(two2, crossed)
    two3 = round_z(two2)
    two2_back = to_sibling(two2)
    two4 = round_z(two3[: 4 * FT])
    two3_back = to_sibling(two3)
    one4_back = to_sibling(one4)
    two4_back = to_sibling(two4)
    out = context_attention(
        info,
        queries,
        state,
        [sibling, partner, partner_sibling]
        + [one1, one1_back, two1, two1_back, one2, one2_back, two2, two2_back]
        + [one3, one3_back, two3, two3_back, one4, one4_back, two4, two4_back],
        CTX,
        everywhere,
        crossed,
    )
    return out[None]


def solution(mesh):
    spec = P("win", None, "head")
    return jax.shard_map(
        on_device, mesh=mesh, in_specs=(spec, spec, spec, P(), P()), out_specs=spec, check_vma=False
    )
```

time: 147 us -> 129 us (0.88)
  waiting for transfers between devices: 68.4 us -> 53.9 us
  between operations: 14.8 us -> 0.46 us
  starting transfers between devices: 6.5 us -> 18.7 us
  other arithmetic: 8.79 us -> 3.24 us
  Pallas kernels: 41.5 us -> 45.6 us
    all_gather x1 -> x0, waiting for transfers between devices: 61.8 us -> none  [on_device(): frames = lax.all_gather(packed, 'win', axis=0, tiled=True)]
    ppermute x0 -> x19, waiting for transfers between devices: none -> 53.9 us  [moved(): return lax.ppermute(value, 'win', [(i, target(i)) for i in range(peers)])]
    ppermute x0 -> x19, starting transfers between devices: none -> 13.3 us  [moved(): return lax.ppermute(value, 'win', [(i, target(i)) for i in range(peers)])]
    ppermute x2, waiting for transfers between devices: 6.62 us -> 0.01 us  [shifted(): return lax.ppermute(value, 'win', pairs)]
    pallas_call x2 -> x4, Pallas kernels: 34.1 us -> 38.1 us  [the longest x2 18.2 us: own_attention(): pl.pallas_call(kernel, grid=(count,), in_specs=[block] * 3 + untouched, o...]
    unnamed x8 -> x46, local copies, waits for them, and re-layouts: 0.96 us -> 4.23 us
    dynamic_slice x3 -> x1, local copies, waits for them, and re-layouts: 1.96 us -> 0.18 us  [slot_info(): entries = lax.dynamic_index_in_dim(context_index, win_id, 0, keepdims=False)]
  transfers between devices with their start and end apart: 3 -> 21, of which waited for: 2 -> 10; matrix products, arithmetic and copies ran while one was open for 6% -> 2% of each run, Pallas kernels for 16% -> 20%
where the time goes in v2:
time: 129 us; the launch traced here: 127 us
  waiting for transfers between devices  53.9 us (42%)
  Pallas kernels  45.6 us (35%)
  starting transfers between devices  18.7 us (14%)
  local copies, waits for them, and re-layouts  5.31 us (4%)
  other arithmetic  3.24 us (3%)
    ppermute x19, waiting for transfers between devices, moved(): return lax.ppermute(value, 'win', [(i, target(i)) for i in range(peers)])  53.9 us
    pallas_call x2, Pallas kernels, own_attention(): pl.pallas_call(kernel, grid=(count,), in_specs=[block] * 3 + untouched, o...  18.2 us
    pallas_call x1, Pallas kernels, context_attention(): pl.pallas_call(functools.partial(context_kernel, tile=192, most=most, sou...  17 us
    ppermute x19, starting transfers between devices, moved(): return lax.ppermute(value, 'win', [(i, target(i)) for i in range(peers)])  13.3 us
    pallas_call x1, Pallas kernels, cross_attention(): pl.pallas_call(functools.partial(cross_kernel, tile=384), grid_spec=pltpu...  7.43 us
    ppermute x2, starting transfers between devices, shifted(): return lax.ppermute(value, 'win', pairs)  5.32 us
    unnamed x46, local copies, waits for them, and re-layouts  4.23 us
    pallas_call x1, Pallas kernels, packed(): pl.pallas_call(pack_kernel, in_specs=[pl.BlockSpec(memory_space=pltpu.VME...  2.93 us
  transfers between devices with their start and end apart: 21, of which 10 were waited for; matrix products, arithmetic and copies ran while one was open for 2% of the time, Pallas kernels for 20%

profile of v2, /device:TPU:1, one launch (start us, length us, event | category | flops | bytes accessed | tf_op | source)
XLA Modules:
  0.0 127.1 jit_solution(11615705892018512484)
XLA Ops:
  0.0 1.4 %copy.12.index_ref = s32[32,16]{1,0:T(8,128)} copy(s32[32,16]{0,1:T(8,128)} %param.8) | data formatting | bytes 4096 | tf_op args[3]
  1.4 2.9 %pack.1 = bf16[384,640]{1,0:T(8,128)(2,1)} custom-call(s32[32,16]{1,0:T(8,128)} %copy.12.index_ref, bf16[1152,640]{1,0:T(8,128)(2,1)} %bitcast.18, bf16[1152,640]{1,0:T(8,128)(2,1)} %bitcast.21), custom_call_target="tpu_custom_call" | custom-call | tf_op jit(solution)/shard_map/pack/pallas_call | solution.py:361
  4.3 3.3 %collective-permute-start = (bf16[384,640]{1,0:T(8,128)(2,1)}, bf16[384,640]{1,0:T(8,128)(2,1)S(1)}, u32[]{:S(2)}, u32[]{:S(2)}) collective-permute-start(bf16[384,640]{1,0:T(8,128)(2,1)} %pack.1), channel_id=1, source_target_pairs={{0,8},{8,0},{16,24},{24,16},{32,40},{40,32},{48,56},{56,48},{64,72... | collective-permute-start | bytes 1474568 | tf_op jit(solution)/shard_map/ppermute | solution.py:316
  7.7 1.7 %collective-permute-done.refs_1_ = bf16[384,640]{1,0:T(8,128)(2,1)S(1)} collective-permute-done((bf16[384,640]{1,0:T(8,128)(2,1)}, bf16[384,640]{1,0:T(8,128)(2,1)S(1)}, u32[]{:S(2)}, u32[]{:S(2)}) %collective-permute-start) | collective-permute-done | bytes 491552 | tf_op jit(solution)/shard_map/ppermute | solution.py:316
  9.4 1.3 %pad_maximum_fusion = bf16[768,640]{1,0:T(8,128)(2,1)S(1)} fusion(bf16[384,640]{1,0:T(8,128)(2,1)S(1)} %collective-permute-done.refs_1_, bf16[384,640]{1,0:T(8,128)(2,1)} %pack.1), kind=kLoop, calls=%fused_computation | loop fusion | flops 1966080 | bytes 1966080 | tf_op jit(solution)/shard_map/concatenate | solution.py:391
  10.7 3.9 %collective-permute-start.1 = (bf16[768,640]{1,0:T(8,128)(2,1)S(1)}, bf16[768,640]{1,0:T(8,128)(2,1)S(1)}, u32[]{:S(2)}, u32[]{:S(2)}) collective-permute-start(bf16[768,640]{1,0:T(8,128)(2,1)S(1)} %pad_maximum_fusion), channel_id=1, source_target_pairs={{0,32},{8,232},{16,48},{24,248},{32,64},{40,8},{48,80},{56,24},{64... | collective-permute-start | bytes 2949128 | tf_op jit(solution)/shard_map/ppermute | solution.py:316
  14.6 1.2 collective-permute-start.2
  16.0 1.5 %pad_maximum_fusion.1 = (bf16[768,640]{1,0:T(8,128)(2,1)}, bf16[768,640]{1,0:T(8,128)(2,1)}) fusion(bf16[384,640]{1,0:T(8,128)(2,1)S(1)} %get-tuple-element.48, bf16[384,640]{1,0:T(8,128)(2,1)S(1)} %get-tuple-element.46, bf16[384,640]{1,0:T(8,128)(2,1)S(1)} %get-tuple-element.47, bf16[384,640]{1,0:T(8,128)(2,1)S(1)} %get-tuple-element.45), kind=kLoop, calls=%fused_computation.1 | loop fusion | flops 3932160 | bytes 3932160 | tf_op jit(solution)/shard_map/concatenate | solution.py:393
  17.5 10.5 %own.2 = (f32[1152,640]{1,0:T(8,128)}, f32[1152,640]{1,0:T(8,128)}) custom-call(bf16[1152,640]{1,0:T(8,128)(2,1)} %bitcast.14, bf16[1152,640]{1,0:T(8,128)(2,1)} %bitcast.19, bf16[1152,640]{1,0:T(8,128)(2,1)} %bitcast.22), custom_call_target="tpu_custom_call" | custom-call | flops 200000000 | tf_op jit(solution)/shard_map/own/pallas_call | solution.py:75
  28.2 1.8 %collective-permute-done.4.refs_3_ = bf16[384,640]{1,0:T(8,128)(2,1)S(1)} collective-permute-done((bf16[384,640]{1,0:T(8,128)(2,1)S(1)}, bf16[384,640]{1,0:T(8,128)(2,1)S(1)}, u32[]{:S(2)}, u32[]{:S(2)}) %collective-permute-start.4) | collective-permute-done | bytes 491552 | tf_op jit(solution)/shard_map/ppermute | solution.py:316
  30.0 0.8 collective-permute-start.5
  30.8 1.3 %collective-permute-start.3 = (bf16[768,640]{1,0:T(8,128)(2,1)S(1)}, bf16[768,640]{1,0:T(8,128)(2,1)}, u32[]{:S(2)}, u32[]{:S(2)}) collective-permute-start(bf16[768,640]{1,0:T(8,128)(2,1)S(1)} %collective-permute-done.1.refs_4_), channel_id=1, source_target_pairs={{0,32},{8,232},{16,48},{24,248},{32,64},{40,8},{48,80},{56,24},{64... | collective-permute-start | bytes 2949128 | tf_op jit(solution)/shard_map/ppermute | solution.py:316
  32.1 1.9 %collective-permute-start.7 = (bf16[768,640]{1,0:T(8,128)(2,1)}, bf16[768,640]{1,0:T(8,128)(2,1)}, u32[]{:S(2)}, u32[]{:S(2)}) collective-permute-start(bf16[768,640]{1,0:T(8,128)(2,1)} %get-tuple-element.38), channel_id=1, source_target_pairs={{0,8},{8,16},{16,24},{24,32},{32,40},{40,48},{48,56},{56,64},{64,7... | collective-permute-start | bytes 2949128 | tf_op jit(solution)/shard_map/ppermute | solution.py:334
  34.0 3.4 %collective-permute-start.8 = (bf16[768,640]{1,0:T(8,128)(2,1)}, bf16[768,640]{1,0:T(8,128)(2,1)}, u32[]{:S(2)}, u32[]{:S(2)}) collective-permute-start(bf16[768,640]{1,0:T(8,128)(2,1)} %get-tuple-element.39), channel_id=1, source_target_pairs={{8,0},{16,8},{24,16},{32,24},{40,32},{48,40},{56,48},{64,56},{72,6... | collective-permute-start | bytes 2949128 | tf_op jit(solution)/shard_map/ppermute | solution.py:334
  37.5 7.3 %collective-permute-done.5.refs_6_ = bf16[768,640]{1,0:T(8,128)(2,1)S(1)} collective-permute-done((bf16[768,640]{1,0:T(8,128)(2,1)S(1)}, bf16[768,640]{1,0:T(8,128)(2,1)S(1)}, u32[]{:S(2)}, u32[]{:S(2)}) %collective-permute-start.5) | collective-permute-done | bytes 983072 | tf_op jit(solution)/shard_map/ppermute | solution.py:316
  44.8 0.9 collective-permute-start.6
  46.3 0.6 concatenate.15.info
  46.9 7.8 %own.3 = (f32[1152,640]{1,0:T(8,128)}, f32[1152,640]{1,0:T(8,128)}) custom-call(bf16[1152,640]{1,0:T(8,128)(2,1)} %bitcast.15, bf16[1152,640]{1,0:T(8,128)(2,1)} %bitcast.20, bf16[1152,640]{1,0:T(8,128)(2,1)} %bitcast.23, f32[1152,640]{1,0:T(8,128)} %get-tuple-element.32.refs_0_, ...), custom_call_target="tpu_custom_call", output_to_operand_aliasing={{0}: (3, {}), {1}: (4, {})} | custom-call | flops 140000000 | tf_op jit(solution)/shard_map/own/pallas_call | solution.py:75
  54.6 9.9 %collective-permute-done.3.refs_8_ = bf16[768,640]{1,0:T(8,128)(2,1)} collective-permute-done((bf16[768,640]{1,0:T(8,128)(2,1)S(1)}, bf16[768,640]{1,0:T(8,128)(2,1)}, u32[]{:S(2)}, u32[]{:S(2)}) %collective-permute-start.3) | collective-permute-done | bytes 983072 | tf_op jit(solution)/shard_map/ppermute | solution.py:316
  64.5 7.4 %cross.1.refs_0_ = f32[768,640]{1,0:T(8,128)} custom-call(s32[66]{0:T(128)} %concatenate.15.info, bf16[1152,640]{1,0:T(8,128)(2,1)} %bitcast.16, bf16[768,640]{1,0:T(8,128)(2,1)} %collective-permute-done.7.left_ref, bf16[768,640]{1,0:T(8,128)(2,1)} %collective-permute-done.8.right_ref), custom_call_target="tpu_custom_call" | custom-call | flops 150000000 | tf_op jit(solution)/shard_map/cross/pallas_call | solution.py:111
  72.0 3.0 %collective-permute-done.6.refs_10_ = bf16[768,640]{1,0:T(8,128)(2,1)} collective-permute-done((bf16[768,640]{1,0:T(8,128)(2,1)S(1)}, bf16[768,640]{1,0:T(8,128)(2,1)}, u32[]{:S(2)}, u32[]{:S(2)}) %collective-permute-start.6) | collective-permute-done | bytes 983072 | tf_op jit(solution)/shard_map/ppermute | solution.py:316
  75.0 0.5 collective-permute-start.11
  75.6 9.9 %collective-permute-done.13.refs_12_ = bf16[768,640]{1,0:T(8,128)(2,1)S(1)} collective-permute-done((bf16[768,640]{1,0:T(8,128)(2,1)}, bf16[768,640]{1,0:T(8,128)(2,1)S(1)}, u32[]{:S(2)}, u32[]{:S(2)}) %collective-permute-start.13) | collective-permute-done | bytes 983072 | tf_op jit(solution)/shard_map/ppermute | solution.py:316
  85.6 10.1 %collective-permute-done.15.refs_14_ = bf16[768,640]{1,0:T(8,128)(2,1)S(1)} collective-permute-done((bf16[768,640]{1,0:T(8,128)(2,1)}, bf16[768,640]{1,0:T(8,128)(2,1)S(1)}, u32[]{:S(2)}, u32[]{:S(2)}) %collective-permute-start.15) | collective-permute-done | bytes 983072 | tf_op jit(solution)/shard_map/ppermute | solution.py:316
  95.8 0.6 collective-permute-start.12
  96.6 4.7 %collective-permute-done.17.refs_16_ = bf16[384,640]{1,0:T(8,128)(2,1)S(1)} collective-permute-done((bf16[384,640]{1,0:T(8,128)(2,1)S(1)}, bf16[384,640]{1,0:T(8,128)(2,1)S(1)}, u32[]{:S(2)}, u32[]{:S(2)}) %collective-permute-start.17) | collective-permute-done | bytes 491552 | tf_op jit(solution)/shard_map/ppermute | solution.py:316
  101.3 5.0 %collective-permute-done.19.refs_18_ = bf16[384,640]{1,0:T(8,128)(2,1)S(1)} collective-permute-done((bf16[384,640]{1,0:T(8,128)(2,1)S(1)}, bf16[384,640]{1,0:T(8,128)(2,1)S(1)}, u32[]{:S(2)}, u32[]{:S(2)}) %collective-permute-start.19) | collective-permute-done | bytes 491552 | tf_op jit(solution)/shard_map/ppermute | solution.py:316
  106.6 1.0 copy-done.13
  107.5 0.6 collective-permute-done.20.refs_19_
  108.1 0.8 copy-done.19
  109.0 1.0 copy-done.15
  109.9 17.0 %context.1 = bf16[1152,640]{1,0:T(8,128)(2,1)} custom-call(s32[66]{0:T(128)} %concatenate.15.info, bf16[1152,640]{1,0:T(8,128)(2,1)} %bitcast.17, f32[1152,640]{1,0:T(8,128)} %get-tuple-element.36.own_ref, f32[1152,640]{1,0:T(8,128)} %get-tuple-element.37.lse_ref, f32[768,640]{1,0:T(8,128)} %cross.1.refs_0_, bf16[384,640]{1,0:T(8,128)(2,1)} %copy-done.6, ...), custom_call_target="tpu_custom_call" | custom-call | flops 340000000 | tf_op jit(solution)/shard_map/context/pallas_call | solution.py:278
  (72 shorter events, 1.9 us)
Async XLA Ops:
  1.4 14.4 %copy-start = (bf16[1,1152,640]{2,1,0:T(8,128)(2,1)S(1)}, bf16[1,1152,640]{2,1,0:T(8,128)(2,1)}, u32[]{:S(2)}) copy-start(bf16[1,1152,640]{2,1,0:T(8,128)(2,1)} %param.6) | copy-start | bytes 4423684
  4.3 5.0 %collective-permute-start = (bf16[384,640]{1,0:T(8,128)(2,1)}, bf16[384,640]{1,0:T(8,128)(2,1)S(1)}, u32[]{:S(2)}, u32[]{:S(2)}) collective-permute-start(bf16[384,640]{1,0:T(8,128)(2,1)} %pack.1), channel_id=1, source_target_pairs={{0,8},{8,0},{16,24},{24,16},{32,40},{40,32},{48,56},{56,48},{64,72... | collective-permute-start | bytes 1474568 | tf_op jit(solution)/shard_map/ppermute | solution.py:316
  10.7 17.3 %collective-permute-start.1 = (bf16[768,640]{1,0:T(8,128)(2,1)S(1)}, bf16[768,640]{1,0:T(8,128)(2,1)S(1)}, u32[]{:S(2)}, u32[]{:S(2)}) collective-permute-start(bf16[768,640]{1,0:T(8,128)(2,1)S(1)} %pad_maximum_fusion), channel_id=1, source_target_pairs={{0,32},{8,232},{16,48},{24,248},{32,64},{40,8},{48,80},{56,24},{64... | collective-permute-start | bytes 2949128 | tf_op jit(solution)/shard_map/ppermute | solution.py:316
  14.6 13.4 %collective-permute-start.2 = (bf16[384,640]{1,0:T(8,128)(2,1)S(1)}, bf16[384,640]{1,0:T(8,128)(2,1)S(1)}, u32[]{:S(2)}, u32[]{:S(2)}) collective-permute-start(bf16[384,640]{1,0:T(8,128)(2,1)S(1)} %copy-done.7), channel_id=1, source_target_pairs={{0,16},{8,24},{16,0},{24,8},{32,48},{40,56},{48,32},{56,40},{64,80... | collective-permute-start | bytes 1474568 | tf_op jit(solution)/shard_map/ppermute | solution.py:316
  28.0 17.7 %copy-start.20 = (s32[32,16]{0,1:T(8,128)S(1)}, s32[32,16]{0,1:T(8,128)}, u32[]{:S(2)}) copy-start(s32[32,16]{0,1:T(8,128)} %param.8) | copy-start | bytes 6148
  28.0 18.3 %copy-start.21 = (s32[32]{0:T(128)S(1)}, s32[32]{0:T(128)}, u32[]{:S(2)}) copy-start(s32[32]{0:T(128)} %param.9) | copy-start | bytes 388
  28.0 26.7 %copy-start.4 = (bf16[384,640]{1,0:T(8,128)(2,1)}, bf16[384,640]{1,0:T(8,128)(2,1)S(1)}, u32[]{:S(2)}) copy-start(bf16[384,640]{1,0:T(8,128)(2,1)S(1)} %collective-permute-done.2.refs_2_) | copy-start | bytes 1474564
  28.0 47.0 %copy-start.8 = (bf16[768,640]{1,0:T(8,128)(2,1)}, bf16[768,640]{1,0:T(8,128)(2,1)S(1)}, u32[]{:S(2)}) copy-start(bf16[768,640]{1,0:T(8,128)(2,1)S(1)} %collective-permute-done.1.refs_4_) | copy-start | bytes 2949124
  28.0 2.0 %collective-permute-start.4 = (bf16[384,640]{1,0:T(8,128)(2,1)S(1)}, bf16[384,640]{1,0:T(8,128)(2,1)S(1)}, u32[]{:S(2)}, u32[]{:S(2)}) collective-permute-start(bf16[384,640]{1,0:T(8,128)(2,1)S(1)} %collective-permute-done.2.refs_2_), channel_id=1, source_target_pairs={{0,8},{8,0},{16,24},{24,16},{32,40},{40,32},{48,56},{56,48},{64,72... | collective-permute-start | bytes 1474568 | tf_op jit(solution)/shard_map/ppermute | solution.py:316
  30.0 24.7 %copy-start.5 = (bf16[384,640]{1,0:T(8,128)(2,1)}, bf16[384,640]{1,0:T(8,128)(2,1)S(1)}, u32[]{:S(2)}) copy-start(bf16[384,640]{1,0:T(8,128)(2,1)S(1)} %collective-permute-done.4.refs_3_) | copy-start | bytes 1474564
  30.0 14.7 %collective-permute-start.5 = (bf16[768,640]{1,0:T(8,128)(2,1)S(1)}, bf16[768,640]{1,0:T(8,128)(2,1)S(1)}, u32[]{:S(2)}, u32[]{:S(2)}) collective-permute-start(bf16[768,640]{1,0:T(8,128)(2,1)S(1)} %constant_dynamic-update-slice_fusion), channel_id=1, source_target_pairs={{0,32},{8,232},{16,48},{24,248},{32,64},{40,8},{48,80},{56,24},{64... | collective-permute-start | bytes 2949128 | tf_op jit(solution)/shard_map/ppermute | solution.py:316
  30.8 33.7 %collective-permute-start.3 = (bf16[768,640]{1,0:T(8,128)(2,1)S(1)}, bf16[768,640]{1,0:T(8,128)(2,1)}, u32[]{:S(2)}, u32[]{:S(2)}) collective-permute-start(bf16[768,640]{1,0:T(8,128)(2,1)S(1)} %collective-permute-done.1.refs_4_), channel_id=1, source_target_pairs={{0,32},{8,232},{16,48},{24,248},{32,64},{40,8},{48,80},{56,24},{64... | collective-permute-start | bytes 2949128 | tf_op jit(solution)/shard_map/ppermute | solution.py:316
  32.1 32.4 %collective-permute-start.7 = (bf16[768,640]{1,0:T(8,128)(2,1)}, bf16[768,640]{1,0:T(8,128)(2,1)}, u32[]{:S(2)}, u32[]{:S(2)}) collective-permute-start(bf16[768,640]{1,0:T(8,128)(2,1)} %get-tuple-element.38), channel_id=1, source_target_pairs={{0,8},{8,16},{16,24},{24,32},{32,40},{40,48},{48,56},{56,64},{64,7... | collective-permute-start | bytes 2949128 | tf_op jit(solution)/shard_map/ppermute | solution.py:334
  34.0 30.5 %collective-permute-start.8 = (bf16[768,640]{1,0:T(8,128)(2,1)}, bf16[768,640]{1,0:T(8,128)(2,1)}, u32[]{:S(2)}, u32[]{:S(2)}) collective-permute-start(bf16[768,640]{1,0:T(8,128)(2,1)} %get-tuple-element.39), channel_id=1, source_target_pairs={{8,0},{16,8},{24,16},{32,24},{40,32},{48,40},{56,48},{64,56},{72,6... | collective-permute-start | bytes 2949128 | tf_op jit(solution)/shard_map/ppermute | solution.py:334
  44.8 30.7 %copy-start.9 = (bf16[768,640]{1,0:T(8,128)(2,1)}, bf16[768,640]{1,0:T(8,128)(2,1)S(1)}, u32[]{:S(2)}) copy-start(bf16[768,640]{1,0:T(8,128)(2,1)S(1)} %collective-permute-done.5.refs_6_) | copy-start | bytes 2949124
  44.8 30.2 %collective-permute-start.6 = (bf16[768,640]{1,0:T(8,128)(2,1)S(1)}, bf16[768,640]{1,0:T(8,128)(2,1)}, u32[]{:S(2)}, u32[]{:S(2)}) collective-permute-start(bf16[768,640]{1,0:T(8,128)(2,1)S(1)} %collective-permute-done.5.refs_6_), channel_id=1, source_target_pairs={{0,32},{8,232},{16,48},{24,248},{32,64},{40,8},{48,80},{56,24},{64... | collective-permute-start | bytes 2949128 | tf_op jit(solution)/shard_map/ppermute | solution.py:316
  64.5 21.0 %collective-permute-start.13 = (bf16[768,640]{1,0:T(8,128)(2,1)}, bf16[768,640]{1,0:T(8,128)(2,1)S(1)}, u32[]{:S(2)}, u32[]{:S(2)}) collective-permute-start(bf16[768,640]{1,0:T(8,128)(2,1)} %collective-permute-done.3.refs_8_), channel_id=1, source_target_pairs={{0,32},{8,232},{16,48},{24,248},{32,64},{40,8},{48,80},{56,24},{64... | collective-permute-start | bytes 2949128 | tf_op jit(solution)/shard_map/ppermute | solution.py:316
  74.9 20.8 %collective-permute-start.15 = (bf16[768,640]{1,0:T(8,128)(2,1)}, bf16[768,640]{1,0:T(8,128)(2,1)S(1)}, u32[]{:S(2)}, u32[]{:S(2)}) collective-permute-start(bf16[768,640]{1,0:T(8,128)(2,1)} %collective-permute-done.6.refs_10_), channel_id=1, source_target_pairs={{0,32},{8,232},{16,48},{24,248},{32,64},{40,8},{48,80},{56,24},{64... | collective-permute-start | bytes 2949128 | tf_op jit(solution)/shard_map/ppermute | solution.py:316
  74.9 20.8 %collective-permute-start.9 = (bf16[768,640]{1,0:T(8,128)(2,1)S(1)}, bf16[768,640]{1,0:T(8,128)(2,1)S(1)}, u32[]{:S(2)}, u32[]{:S(2)}) collective-permute-start(bf16[768,640]{1,0:T(8,128)(2,1)S(1)} %collective-permute-done.1.refs_4_), channel_id=1, source_target_pairs={{0,8},{8,0},{16,24},{24,16},{32,40},{40,32},{48,56},{56,48},{64,72... | collective-permute-start | bytes 2949128 | tf_op jit(solution)/shard_map/ppermute | solution.py:316
  75.0 21.4 %collective-permute-start.11 = (bf16[768,640]{1,0:T(8,128)(2,1)}, bf16[768,640]{1,0:T(8,128)(2,1)S(1)}, u32[]{:S(2)}, u32[]{:S(2)}) collective-permute-start(bf16[768,640]{1,0:T(8,128)(2,1)} %collective-permute-done.3.refs_8_), channel_id=1, source_target_pairs={{0,8},{8,0},{16,24},{24,16},{32,40},{40,32},{48,56},{56,48},{64,72... | collective-permute-start | bytes 2949128 | tf_op jit(solution)/shard_map/ppermute | solution.py:316
  75.5 21.2 %collective-permute-start.10 = (bf16[768,640]{1,0:T(8,128)(2,1)S(1)}, bf16[768,640]{1,0:T(8,128)(2,1)S(1)}, u32[]{:S(2)}, u32[]{:S(2)}) collective-permute-start(bf16[768,640]{1,0:T(8,128)(2,1)S(1)} %collective-permute-done.5.refs_6_), channel_id=1, source_target_pairs={{0,8},{8,0},{16,24},{24,16},{32,40},{40,32},{48,56},{56,48},{64,72... | collective-permute-start | bytes 2949128 | tf_op jit(solution)/shard_map/ppermute | solution.py:316
  85.5 23.4 %copy-start.2 = (bf16[768,640]{1,0:T(8,128)(2,1)}, bf16[768,640]{1,0:T(8,128)(2,1)S(1)}, u32[]{:S(2)}) copy-start(bf16[768,640]{1,0:T(8,128)(2,1)S(1)} %collective-permute-done.13.refs_12_) | copy-start | bytes 2949124
  85.5 15.8 %collective-permute-start.17 = (bf16[384,640]{1,0:T(8,128)(2,1)S(1)}, bf16[384,640]{1,0:T(8,128)(2,1)S(1)}, u32[]{:S(2)}, u32[]{:S(2)}) collective-permute-start(bf16[384,640]{1,0:T(8,128)(2,1)S(1)} %slice.40), channel_id=1, source_target_pairs={{0,32},{8,232},{16,48},{24,248},{32,64},{40,8},{48,80},{56,24},{64... | collective-permute-start | bytes 1474568 | tf_op jit(solution)/shard_map/ppermute | solution.py:316
  95.7 13.2 %copy-start.3 = (bf16[768,640]{1,0:T(8,128)(2,1)}, bf16[768,640]{1,0:T(8,128)(2,1)S(1)}, u32[]{:S(2)}) copy-start(bf16[768,640]{1,0:T(8,128)(2,1)S(1)} %collective-permute-done.15.refs_14_) | copy-start | bytes 2949124
  95.7 10.8 %collective-permute-start.14 = (bf16[768,640]{1,0:T(8,128)(2,1)S(1)}, bf16[768,640]{1,0:T(8,128)(2,1)S(1)}, u32[]{:S(2)}, u32[]{:S(2)}) collective-permute-start(bf16[768,640]{1,0:T(8,128)(2,1)S(1)} %collective-permute-done.13.refs_12_), channel_id=1, source_target_pairs={{0,8},{8,0},{16,24},{24,16},{32,40},{40,32},{48,56},{56,48},{64,72... | collective-permute-start | bytes 2949128 | tf_op jit(solution)/shard_map/ppermute | solution.py:316
  95.8 13.1 %copy-start.10 = (bf16[768,640]{1,0:T(8,128)(2,1)}, bf16[768,640]{1,0:T(8,128)(2,1)S(1)}, u32[]{:S(2)}) copy-start(bf16[768,640]{1,0:T(8,128)(2,1)S(1)} %collective-permute-done.9.refs_5_) | copy-start | bytes 2949124
  95.8 11.8 %collective-permute-start.12 = (bf16[768,640]{1,0:T(8,128)(2,1)}, bf16[768,640]{1,0:T(8,128)(2,1)S(1)}, u32[]{:S(2)}, u32[]{:S(2)}) collective-permute-start(bf16[768,640]{1,0:T(8,128)(2,1)} %collective-permute-done.6.refs_10_), channel_id=1, source_target_pairs={{0,8},{8,0},{16,24},{24,16},{32,40},{40,32},{48,56},{56,48},{64,72... | collective-permute-start | bytes 2949128 | tf_op jit(solution)/shard_map/ppermute | solution.py:316
  96.4 12.5 %copy-start.11 = (bf16[768,640]{1,0:T(8,128)(2,1)}, bf16[768,640]{1,0:T(8,128)(2,1)S(1)}, u32[]{:S(2)}) copy-start(bf16[768,640]{1,0:T(8,128)(2,1)S(1)} %collective-permute-done.11.refs_9_) | copy-start | bytes 2949124
  96.4 9.9 %collective-permute-start.19 = (bf16[384,640]{1,0:T(8,128)(2,1)S(1)}, bf16[384,640]{1,0:T(8,128)(2,1)S(1)}, u32[]{:S(2)}, u32[]{:S(2)}) collective-permute-start(bf16[384,640]{1,0:T(8,128)(2,1)S(1)} %slice.41), channel_id=1, source_target_pairs={{0,32},{8,232},{16,48},{24,248},{32,64},{40,8},{48,80},{56,24},{64... | collective-permute-start | bytes 1474568 | tf_op jit(solution)/shard_map/ppermute | solution.py:316
  96.6 12.3 %collective-permute-start.16 = (bf16[768,640]{1,0:T(8,128)(2,1)S(1)}, bf16[768,640]{1,0:T(8,128)(2,1)S(1)}, u32[]{:S(2)}, u32[]{:S(2)}) collective-permute-start(bf16[768,640]{1,0:T(8,128)(2,1)S(1)} %collective-permute-done.15.refs_14_), channel_id=1, source_target_pairs={{0,8},{8,0},{16,24},{24,16},{32,40},{40,32},{48,56},{56,48},{64,72... | collective-permute-start | bytes 2949128 | tf_op jit(solution)/shard_map/ppermute | solution.py:316
  101.3 5.3 %collective-permute-start.18 = (bf16[384,640]{1,0:T(8,128)(2,1)S(1)}, bf16[384,640]{1,0:T(8,128)(2,1)S(1)}, u32[]{:S(2)}, u32[]{:S(2)}) collective-permute-start(bf16[384,640]{1,0:T(8,128)(2,1)S(1)} %collective-permute-done.17.refs_16_), channel_id=1, source_target_pairs={{0,8},{8,0},{16,24},{24,16},{32,40},{40,32},{48,56},{56,48},{64,72... | collective-permute-start | bytes 1474568 | tf_op jit(solution)/shard_map/ppermute | solution.py:316
  106.2 1.9 %collective-permute-start.20 = (bf16[384,640]{1,0:T(8,128)(2,1)S(1)}, bf16[384,640]{1,0:T(8,128)(2,1)S(1)}, u32[]{:S(2)}, u32[]{:S(2)}) collective-permute-start(bf16[384,640]{1,0:T(8,128)(2,1)S(1)} %collective-permute-done.19.refs_18_), channel_id=1, source_target_pairs={{0,8},{8,0},{16,24},{24,16},{32,40},{40,32},{48,56},{56,48},{64,72... | collective-permute-start | bytes 1474568 | tf_op jit(solution)/shard_map/ppermute | solution.py:316
  (11 other events, 56.3 us)
